TPU v7x, 32 devices: a whole 2x2x4 slice. The times are simulated.
32 devices in a mesh: tok: 8 (over z, y), mp: 4 (over x, core).
Axes of the slice: x: 2, y: 2, z: 4, core: 2. Of those that a mesh axis runs over, the one named last changes fastest.
Arguments:
- tokens: bfloat16 [8192, 2048], P('tok'), may hold values from -6 to 6
- norm_gain: float32 [2048], replicated, may hold values from 0.1 to 1.9
- w_query: bfloat16 [2048, 2048], P(None, 'mp'), may hold values from -2 to 2
- w_key: bfloat16 [2048, 2048], P(None, 'mp'), may hold values from -2 to 2
- w_value: bfloat16 [2048, 2048], P(None, 'mp'), may hold values from -0.125 to 0.125
- w_out: bfloat16 [2048, 2048], replicated, may hold values from -2.5 to 2.5
- kv_cache: bfloat16 [2, 8192, 2, 2048], P(None, 'tok', None, 'mp'), may hold values from -6 to 6
- wake_blocks: int32 [64, 8], replicated, may hold values from 0 to 63, as said below
- wake_frames: int32 [64, 8], replicated, may hold values from 0 to 1
- wake_counts: int32 [64], replicated, may hold values from 2 to 8, as said below
Outputs:
- advanced: bfloat16 [8192, 2048], P('tok', 'mp')
Inputs may be any that keep to these rules, and one draw needn't show every extreme that they name: `wake_blocks`: blocks i * 8 to (i + 1) * 8 - 1 are held by tok index i. Among the live slots (w below the block's count) of the 8 query blocks of one tok index, at most 8 name blocks held by any one tok index, and for every tok index some holder is named exactly 8 times. Slots at or past the count hold any block number. `wake_counts`: some query block has all 8 slots live.
All inputs are finite; a program needn't handle non-finite values.
Results may differ from a plain program's by a relative error of at most 0.005.
The roundings to bfloat16 on the way count: a program that leaves them out, or rounds other values in their place, can miss the bound.
Values may be sent and summed in bfloat16 or wider, within the bound.
A program may use at most 192 MiB of HBM per device.

v0:
```python
import math

import jax
import jax.numpy as jnp
from jax import lax
from jax.sharding import PartitionSpec as P

HEAD_DIM = 128
BLOCK = 128
WMAX = 8


def with_halo(block, sides, width):
    for axis, dim in sides:
        count = lax.axis_size(axis)
        forward = [(i, i + 1) for i in range(count - 1)]
        forward.append((count - 1, 0))
        backward = [(target, source) for source, target in forward]
        low = lax.ppermute(
            lax.slice_in_dim(block, block.shape[dim] - width, None, axis=dim), axis, forward
        )
        high = lax.ppermute(lax.slice_in_dim(block, 0, width, axis=dim), axis, backward)
        block = jnp.concatenate([low, block, high], axis=dim)
    return block


def on_device(
    tokens,
    norm_gain,
    w_query,
    w_key,
    w_value,
    w_out,
    kv_cache,
    wake_blocks,
    wake_frames,
    wake_counts,
):
    tok_rows = tokens.shape[0]
    local_width = w_query.shape[1]
    head_count = local_width // HEAD_DIM
    blocks_dev = tok_rows // BLOCK
    slot_count = blocks_dev * WMAX
    tok_devices = lax.axis_size("tok")
    capacity = max(2, (slot_count + tok_devices - 1) // tok_devices)
    tok_place = lax.axis_index("tok")
    model_place = lax.axis_index("mp")
    tokens_f32 = tokens.astype(jnp.float32)
    inverse = lax.rsqrt(jnp.mean(tokens_f32 * tokens_f32, axis=1, keepdims=True) + 1e-05)
    normed = (tokens_f32 * inverse * norm_gain[None, :]).astype(jnp.bfloat16)
    queries = jnp.dot(normed, w_query, preferred_element_type=jnp.float32).astype(jnp.bfloat16)
    keys_now = jnp.dot(normed, w_key, preferred_element_type=jnp.float32).astype(jnp.bfloat16)
    values_now = jnp.dot(normed, w_value, preferred_element_type=jnp.float32).astype(jnp.bfloat16)
    current = jnp.concatenate([keys_now, values_now], axis=1)
    extended = with_halo(current, (("tok", 0),), BLOCK)
    local_rows = jnp.concatenate(
        [
            extended[offset * BLOCK : offset * BLOCK + tok_rows].reshape(
                blocks_dev, BLOCK, 2 * local_width
            )
            for offset in range(3)
        ],
        axis=1,
    )
    all_lists = wake_blocks.reshape(tok_devices, slot_count)
    all_frames = wake_frames.reshape(tok_devices, slot_count)
    all_live = (jnp.arange(WMAX, dtype=jnp.int32)[None, :] < wake_counts[:, None]).reshape(
        tok_devices, slot_count
    )
    held_here = all_live & (all_lists // blocks_dev == tok_place)
    position = jnp.cumsum(held_here.astype(jnp.int32), axis=1) - 1
    picked = held_here[:, None, :] & (
        position[:, None, :] == jnp.arange(capacity, dtype=jnp.int32)[None, :, None]
    )
    local_index = all_frames * blocks_dev + all_lists % blocks_dev
    chosen = jnp.sum(jnp.where(picked, local_index[:, None, :], 0), axis=2)
    cache_table = kv_cache.reshape(kv_cache.shape[0] * blocks_dev, BLOCK, 2 * local_width)
    outgoing = cache_table[chosen]
    incoming = lax.all_to_all(outgoing, "tok", split_axis=0, concat_axis=0, tiled=True)
    my_lists = lax.dynamic_slice_in_dim(all_lists, tok_place, 1, 0).reshape(slot_count)
    my_live = lax.dynamic_slice_in_dim(all_live, tok_place, 1, 0).reshape(slot_count)
    my_owner = my_lists // blocks_dev
    owner_hits = (
        my_live[:, None] & (my_owner[:, None] == jnp.arange(tok_devices, dtype=jnp.int32)[None, :])
    ).astype(jnp.int32)
    my_position = jnp.sum(jnp.cumsum(owner_hits, axis=0) * owner_hits, axis=1) - 1
    slot_index = jnp.where(my_live, my_owner * capacity + my_position, 0)
    wake_rows = incoming.reshape(tok_devices * capacity, BLOCK, 2 * local_width)[slot_index]
    wake_rows = wake_rows.reshape(blocks_dev, WMAX * BLOCK, 2 * local_width)
    every_row = jnp.concatenate([local_rows, wake_rows], axis=1)
    key_count = every_row.shape[1]
    key_part = every_row[:, :, :local_width].reshape(blocks_dev, key_count, head_count, HEAD_DIM)
    value_part = every_row[:, :, local_width:].reshape(blocks_dev, key_count, head_count, HEAD_DIM)
    query_part = queries.reshape(blocks_dev, BLOCK, head_count, HEAD_DIM)
    scores = jnp.einsum(
        "bqhd,bkhd->bhqk", query_part, key_part, preferred_element_type=jnp.float32
    ) * (1.0 / math.sqrt(HEAD_DIM))
    key_live = jnp.concatenate(
        [
            jnp.ones((blocks_dev, 3 * BLOCK), bool),
            jnp.repeat(my_live.reshape(blocks_dev, WMAX), BLOCK, axis=1),
        ],
        axis=1,
    )
    scores = jnp.where(key_live[:, None, None, :], scores, -1e30)
    row_peak = jnp.max(scores, axis=3, keepdims=True)
    shifted = jnp.exp(scores - row_peak)
    weights = (shifted / jnp.sum(shifted, axis=3, keepdims=True)).astype(jnp.bfloat16)
    attention = jnp.einsum(
        "bhqk,bkhd->bqhd", weights, value_part, preferred_element_type=jnp.float32
    )
    attention = attention.astype(jnp.bfloat16).reshape(tok_rows, local_width)
    own_rows = lax.dynamic_slice_in_dim(w_out, model_place * local_width, local_width, 0)
    partial_sum = jnp.dot(attention, own_rows, preferred_element_type=jnp.float32)
    mixed_sum = lax.psum_scatter(partial_sum, "mp", scatter_dimension=1, tiled=True)
    residual_part = lax.dynamic_slice_in_dim(tokens_f32, model_place * local_width, local_width, 1)
    return (residual_part + mixed_sum).astype(jnp.bfloat16)


def solution(mesh):
    return jax.shard_map(
        on_device,
        mesh=mesh,
        in_specs=(
            P("tok", None),
            P(),
            P(None, "mp"),
            P(None, "mp"),
            P(None, "mp"),
            P(),
            P(None, "tok", None, "mp"),
            P(),
            P(),
            P(),
        ),
        out_specs=P("tok", "mp"),
        check_vma=False,
    )
```

profile of v0, /device:TPU:0, one launch (start us, length us, event | category | flops | bytes accessed | tf_op | source)
XLA Modules:
  0.0 618.3 jit_solution(5390702954184676294)
XLA Ops:
  6.5 7.9 %reshape.325 = bf16[16,128,1024]{2,1,0:T(8,128)(2,1)} reshape(bf16[2,1024,2,512]{3,2,1,0:T(2,128)(2,1)} %param.16) | data formatting | bytes 8388608 | tf_op jit(solution)/shard_map/reshape | solution.py:77
  15.1 0.2 reduce_window_sum.22
  15.3 0.2 select_reduce_fusion.1
  15.6 9.6 %gather_fusion = bf16[64,128,1024]{2,1,0:T(8,128)(2,1)} fusion(bf16[16,128,1024]{2,1,0:T(8,128)(2,1)} %reshape.325, s32[1024]{0:T(1024)S(1)} %pad_clamp_fusion.1), kind=kCustom, calls=%fused_computation | custom fusion | bytes 33554688 | tf_op jit(solution)/shard_map/gather | solution.py:78
  25.3 7.3 %all-to-all-start = ((bf16[8,8,128,1024]{3,2,1,0:T(8,128)(2,1)}), bf16[8,8,128,1024]{3,2,1,0:T(8,128)(2,1)}, u32[]{:S(2)}, u32[]{:S(2)}) async-start(bf16[8,8,128,1024]{3,2,1,0:T(8,128)(2,1)} %bitcast.64), calls=%async_computation | async-start | bytes 33554432 | tf_op jit(solution)/shard_map/all_to_all | solution.py:79
  32.7 3.1 multiply_reduce_fusion
  35.8 4.8 convolution_convert_fusion.2
  40.6 2.6 convolution_convert_fusion.1
  43.2 0.9 fusion.21
  44.1 2.0 collective-permute-start
  46.1 2.7 collective-permute-start.1
  49.2 5.2 convolution_convert_fusion
  54.5 1.3 reshape.334
  55.9 0.2 select_reduce_fusion
  56.1 257.2 %collective-permute-done = bf16[128,1024]{0,1:T(8,128)(2,1)S(1)} collective-permute-done((bf16[128,1024]{0,1:T(8,128)(2,1)}, bf16[128,1024]{0,1:T(8,128)(2,1)S(1)}, u32[]{:S(2)}, u32[]{:S(2)}) %collective-permute-start) | collective-permute-done | bytes 262176 | tf_op jit(solution)/shard_map/ppermute | solution.py:19
  313.3 8.0 %pad_maximum_fusion.4 = (bf16[1024,1024]{0,1:T(8,128)(2,1)}, bf16[1024,1024]{0,1:T(8,128)(2,1)}, bf16[1024,1024]{0,1:T(8,128)(2,1)}) fusion(bf16[128,1024]{0,1:T(8,128)(2,1)S(1)} %collective-permute-done, bf16[1024,512]{0,1:T(8,128)(2,1)S(1)} %convolution_convert_fusion.1, bf16[1024,512]{0,1:T(8,128)(2,1)S(1)} %convolution_convert_fusion.2, ...), kind=kLoop, calls=%fused_computation.23 | loop fusion | flops 16777216 | bytes 8912896 | tf_op jit(solution)/shard_map/concatenate | solution.py:23
  321.4 2.9 copy.43
  324.2 3.9 copy.42
  328.2 4.0 copy.41
  332.1 64.8 %all-to-all-done = bf16[8,8,128,1024]{3,2,1,0:T(8,128)(2,1)} async-done(((bf16[8,8,128,1024]{3,2,1,0:T(8,128)(2,1)}), bf16[8,8,128,1024]{3,2,1,0:T(8,128)(2,1)}, u32[]{:S(2)}, u32[]{:S(2)}) %all-to-all-start) | async-done | bytes 16777248 | tf_op jit(solution)/shard_map/all_to_all | solution.py:79
  397.0 13.1 %gather_fusion.1 = bf16[64,128,1024]{2,1,0:T(8,128)(2,1)} fusion(bf16[64,128,1024]{2,1,0:T(8,128)(2,1)} %bitcast.5, s32[1024]{0:T(1024)S(1)} %pad_clamp_fusion), kind=kCustom, calls=%fused_computation.1 | custom fusion | bytes 33554688 | tf_op jit(solution)/shard_map/gather | solution.py:88
  410.1 22.1 %pad_maximum_fusion = bf16[8,1408,1024]{2,1,0:T(8,128)(2,1)} fusion(bf16[8,1024,1024]{2,1,0:T(8,128)(2,1)} %bitcast.65, bf16[8,128,1024]{2,1,0:T(8,128)(2,1)S(1)} %bitcast.68, bf16[8,128,1024]{2,1,0:T(8,128)(2,1)} %bitcast.69, bf16[8,128,1024]{2,1,0:T(8,128)(2,1)} %bitcast.70), kind=kLoop, calls=%fused_computation.4 | loop fusion | flops 92274688 | bytes 46137344 | tf_op jit(solution)/shard_map/concatenate | solution.py:90
  432.2 16.2 %fusion.39 = (bf16[8,1408,512]{2,1,0:T(8,128)(2,1)}, bf16[8,1408,512]{2,1,0:T(8,128)(2,1)}) fusion(bf16[8,1408,1024]{2,1,0:T(8,128)(2,1)} %pad_maximum_fusion), kind=kLoop, calls=%fused_computation.88 | loop fusion | bytes 46137344 | tf_op jit(solution)/shard_map/slice | solution.py:92
  448.3 15.3 %copy.34 = bf16[8,1408,512]{1,2,0:T(8,128)(2,1)} copy(bf16[8,1408,512]{2,1,0:T(8,128)(2,1)} %get-tuple-element.9) | data formatting | bytes 23068672 | tf_op jit(solution)/shard_map/slice | solution.py:93
  463.6 15.2 %copy.36 = bf16[8,1408,512]{1,2,0:T(8,128)(2,1)} copy(bf16[8,1408,512]{2,1,0:T(8,128)(2,1)} %get-tuple-element.8) | data formatting | bytes 23068672 | tf_op jit(solution)/shard_map/slice | solution.py:92
  478.8 14.8 %exponential_reduce_fusion = (f32[8,4,128]{2,1,0:T(4,128)S(1)}, f32[8,4,128,1408]{3,2,1,0:T(8,128)}) fusion(pred[8,1408]{1,0:T(8,128)(4,1)S(1)} %concatenate.20, bf16[8,1408,4,128]{1,3,2,0:T(8,128)(2,1)} %bitcast.67, bf16[8,128,4,128]{3,2,1,0:T(4,128)(2,1)S(1)} %copy-done.3), kind=kOutput, calls=%fused_computation.7 | convolution fusion | flops 1499465088 | bytes 35679232 | tf_op jit(solution)/shard_map/sub | solution.py:107
  493.6 13.0 %fusion.12 = bf16[8,128,4,128]{1,3,2,0:T(8,128)(2,1)S(1)} fusion(bf16[8,1408,4,128]{1,3,2,0:T(8,128)(2,1)} %bitcast.66, f32[8,4,128,1408]{3,2,1,0:T(8,128)} %get-tuple-element.18, f32[8,4,128]{2,1,0:T(4,128)S(1)} %get-tuple-element.17), kind=kOutput, calls=%fused_computation.32 | convolution fusion | flops 1488453632 | bytes 35667968 | tf_op jit(solution)/shard_map/bhqk,bkhd->bqhd/dot_general | solution.py:109
  506.6 0.7 copy.39
  507.3 7.2 %fusion.9 = f32[1024,2048]{1,0:T(8,128)} fusion(bf16[2048,2048]{1,0:T(8,128)(2,1)} %param.15, s32[]{:T(128)S(6)} %select_n.88, bf16[64,8,8,128]{3,2,1,0:T(8,128)(2,1)S(1)} %bitcast.71), kind=kOutput, calls=%fused_computation.26 | convolution fusion | flops 2147483648 | bytes 11534340 | tf_op jit(solution)/shard_map/dot_general | solution.py:114
  514.6 6.6 %convert_element_type.37 = f32[1024,2048]{1,0:T(8,128)} convert(bf16[1024,2048]{1,0:T(8,128)(2,1)} %param.10) | non-fusion elementwise | flops 2097152 | bytes 12582912 | tf_op jit(solution)/shard_map/convert_element_type | solution.py:48
  521.2 86.8 %reduce-scatter.2.cloned.1.call-done = f32[1024,512]{1,0:T(8,128)} async-done(((f32[1024,2048]{1,0:T(8,128)}), f32[1024,512]{1,0:T(8,128)}) %reduce-scatter.2.cloned.1.call-update) | async-done | bytes 2097168 | tf_op jit(solution)/shard_map/reduce_scatter | solution.py:115
  607.9 3.5 add_convert_fusion
  (47 shorter events, 1.4 us)
Async XLA Ops:
  6.5 29.2 %copy-start = (bf16[2048,512]{1,0:T(8,128)(2,1)S(1)}, bf16[2048,512]{1,0:T(8,128)(2,1)}, u32[]{:S(2)}) copy-start(bf16[2048,512]{1,0:T(8,128)(2,1)} %param.13) | copy-start | bytes 6291460
  6.5 7.9 %copy-start.5 = (s32[64,8]{0,1:T(8,128)S(1)}, s32[64,8]{0,1:T(8,128)}, u32[]{:S(2)}) copy-start(s32[64,8]{0,1:T(8,128)} %param.18) | copy-start | bytes 6148
  6.5 8.0 %copy-start.4 = (s32[64,8]{0,1:T(8,128)S(1)}, s32[64,8]{0,1:T(8,128)}, u32[]{:S(2)}) copy-start(s32[64,8]{0,1:T(8,128)} %param.17) | copy-start | bytes 6148
  6.5 8.2 %copy-start.6 = (s32[64]{0:T(128)S(1)}, s32[64]{0:T(128)}, u32[]{:S(2)}) copy-start(s32[64]{0:T(128)} %param.19) | copy-start | bytes 772
  25.3 10.5 %copy-start.8 = (f32[2048]{0:T(1024)S(1)}, f32[2048]{0:T(1024)}, u32[]{:S(2)}) copy-start(f32[2048]{0:T(1024)} %param.11) | copy-start | bytes 24580
  25.3 371.7 %all-to-all-start = ((bf16[8,8,128,1024]{3,2,1,0:T(8,128)(2,1)}), bf16[8,8,128,1024]{3,2,1,0:T(8,128)(2,1)}, u32[]{:S(2)}, u32[]{:S(2)}) async-start(bf16[8,8,128,1024]{3,2,1,0:T(8,128)(2,1)} %bitcast.64), calls=%async_computation | async-start | bytes 33554432 | tf_op jit(solution)/shard_map/all_to_all | solution.py:79
  32.6 575.3 %reduce-scatter.2.cloned.1.call-start = ((), (), s32[]{:S(2)}) async-start(), calls=%async_computation.2 | async-start | bytes 10485760 | tf_op jit(solution)/shard_map/reduce_scatter | solution.py:115
  35.8 4.9 copy-start.2
  35.8 4.9 copy-start.7
  44.1 269.2 %collective-permute-start = (bf16[128,1024]{0,1:T(8,128)(2,1)}, bf16[128,1024]{0,1:T(8,128)(2,1)S(1)}, u32[]{:S(2)}, u32[]{:S(2)}) collective-permute-start(bf16[128,1024]{0,1:T(8,128)(2,1)} %get-tuple-element.13), channel_id=1, source_target_pairs={{0,4},{4,8},{8,12},{12,16},{16,20},{20,24},{24,28},{28,0},{1,5},{5... | collective-permute-start | bytes 786440 | tf_op jit(solution)/shard_map/ppermute | solution.py:19
  46.1 267.2 %collective-permute-start.1 = (bf16[128,1024]{0,1:T(8,128)(2,1)}, bf16[128,1024]{0,1:T(8,128)(2,1)}, u32[]{:S(2)}, u32[]{:S(2)}) collective-permute-start(bf16[128,1024]{0,1:T(8,128)(2,1)} %get-tuple-element.14), channel_id=1, source_target_pairs={{4,0},{8,4},{12,8},{16,12},{20,16},{24,20},{28,24},{0,28},{5,1},{9... | collective-permute-start | bytes 786440 | tf_op jit(solution)/shard_map/ppermute | solution.py:22
  463.6 15.2 %copy-start.3 = (bf16[8,128,4,128]{3,2,1,0:T(4,128)(2,1)S(1)}, bf16[8,128,4,128]{3,2,1,0:T(4,128)(2,1)}, u32[]{:S(2)}) copy-start(bf16[8,128,4,128]{3,2,1,0:T(4,128)(2,1)} %reshape.334) | copy-start | bytes 3145732
  514.5 96.9 %copy-start.1 = (bf16[2048,512]{1,0:T(8,128)(2,1)S(1)}, bf16[2048,512]{1,0:T(8,128)(2,1)}, u32[]{:S(2)}) copy-start(bf16[2048,512]{1,0:T(8,128)(2,1)} %param.13) | copy-start | bytes 6291460
Sparse Core Ops, SparseCore 0:
  514.7 93.2 reduce-scatter.1
where the time goes:
time: 620 us; the launch traced here: 618 us
  waiting for transfers between devices  409 us (66%)
  local copies, waits for them, and re-layouts  91 us (15%)
  matrix products  47.7 us (8%)
  other arithmetic  45.1 us (7%)
  between operations  13.6 us (2%)
  starting transfers between devices  12.1 us (2%)
    ppermute x1, waiting for transfers between devices, with_halo(): lax.ppermute(lax.slice_in_dim(block, block.shape[dim] - width, None, axis...  257 us
    reduce_scatter x1, waiting for transfers between devices, on_device(): lax.psum_scatter(partial_sum, 'mp', scatter_dimension=1, tiled=True)  86.8 us
    all_to_all x1, waiting for transfers between devices, on_device(): lax.all_to_all(outgoing, 'tok', split_axis=0, concat_axis=0, tiled=True)  64.8 us
    slice x2, local copies, waits for them, and re-layouts, on_device(): every_row[:, :, :local_width]  31.3 us
    concatenate x1, other arithmetic, on_device(): every_row = jnp.concatenate([local_rows, wake_rows], axis=1)  22.1 us
    slice x1, local copies, waits for them, and re-layouts, on_device(): every_row[:, :, local_width:]  15.3 us
    sub x1, matrix products, on_device(): shifted = jnp.exp(scores - row_peak)  14.8 us
    gather x1, local copies, waits for them, and re-layouts, on_device(): incoming.reshape(tok_devices * capacity, BLOCK, 2 * local_width)[slot_index]  13.1 us
  transfers between devices with their start and end apart: 4, of which 3 were waited for; matrix products, arithmetic and copies ran while one was open for 7% of the time, Pallas kernels for 0%

commit v1 on v0

v1 whole, which is shorter than its diff:
```python
import functools
import math

import jax
import jax.numpy as jnp
from jax import lax
from jax.experimental import pallas as pl
from jax.experimental.pallas import tpu as pltpu
from jax.sharding import PartitionSpec as P

HEAD_DIM = 128
BLOCK = 128
WMAX = 8
NEVER = -1e30
SCALE = 1.0 / math.sqrt(HEAD_DIM)
VMEM_BYTES = 40 * 1024 * 1024


def rows_dot(a, b):
    return lax.dot_general(a, b, (((1,), (1,)), ((), ())), preferred_element_type=jnp.float32)


def cols_dot(a, b):
    return lax.dot_general(a, b, (((0,), (0,)), ((), ())), preferred_element_type=jnp.float32)


def head_cols(h):
    return slice(h * HEAD_DIM, (h + 1) * HEAD_DIM)


def near_kernel(heads, q_ref, k0, k1, k2, v0, v1, v2, o_ref, l_ref):
    for h in range(heads):
        cols = head_cols(h)
        q = q_ref[:, cols]
        keys = jnp.concatenate([k0[:, cols], k1[:, cols], k2[:, cols]], axis=0)
        values = jnp.concatenate([v0[:, cols], v1[:, cols], v2[:, cols]], axis=0)
        scores = rows_dot(keys, q) * SCALE
        peak = jnp.max(scores, axis=0, keepdims=True)
        weights = jnp.exp(scores - peak)
        total = jnp.sum(weights, axis=0, keepdims=True)
        out = cols_dot(values, weights.astype(jnp.bfloat16))
        o_ref[0, h] = out / total
        l_ref[0, h : h + 1, :] = peak + jnp.log(total)


def near_attention(queries, keys, values, heads):
    rows, width = queries.shape
    blocks = rows // BLOCK
    spec = [pl.BlockSpec((BLOCK, width), functools.partial(lambda j, b: (b + j, 0), j)) for j in range(3)]
    return pl.pallas_call(
        functools.partial(near_kernel, heads),
        grid=(blocks,),
        in_specs=[pl.BlockSpec((BLOCK, width), lambda b: (b, 0))] + spec + spec,
        out_specs=[
            pl.BlockSpec((1, heads, HEAD_DIM, BLOCK), lambda b: (b, 0, 0, 0)),
            pl.BlockSpec((1, heads, BLOCK), lambda b: (b, 0, 0)),
        ],
        out_shape=[
            jax.ShapeDtypeStruct((blocks, heads, HEAD_DIM, BLOCK), jnp.float32),
            jax.ShapeDtypeStruct((blocks, heads, BLOCK), jnp.float32),
        ],
        compiler_params=pltpu.CompilerParams(vmem_limit_bytes=VMEM_BYTES),
        cost_estimate=pl.CostEstimate(
            flops=4 * rows * 3 * BLOCK * width, bytes_accessed=rows * width * 20, transcendentals=rows * 3 * BLOCK * heads
        ),
    )(queries, keys, keys, keys, values, values, values)


def wake_kernel(heads, idx_ref, cnt_ref, q_ref, table_ref, o_ref, l_ref, acc, peak, total):
    block = pl.program_id(0)
    count = cnt_ref[block]
    width = heads * HEAD_DIM

    @pl.when(count == 0)
    def _():
        o_ref[...] = jnp.zeros_like(o_ref)
        l_ref[...] = jnp.full_like(l_ref, NEVER)

    @pl.when(count > 0)
    def _():
        acc[...] = jnp.zeros_like(acc)
        peak[...] = jnp.full_like(peak, NEVER)
        total[...] = jnp.zeros_like(total)

        def step(s, carry):
            place = idx_ref[block * WMAX + s]
            for h in range(heads):
                cols = head_cols(h)
                keys = table_ref[place, :, cols]
                values = table_ref[place, :, width + h * HEAD_DIM : width + (h + 1) * HEAD_DIM]
                scores = rows_dot(keys, q_ref[0, :, cols]) * SCALE
                old = peak[h : h + 1, :]
                new = jnp.maximum(old, jnp.max(scores, axis=0, keepdims=True))
                weights = jnp.exp(scores - new)
                fade = jnp.exp(old - new)
                peak[h : h + 1, :] = new
                total[h : h + 1, :] = total[h : h + 1, :] * fade + jnp.sum(weights, axis=0, keepdims=True)
                acc[h] = acc[h] * fade + cols_dot(values, weights.astype(jnp.bfloat16))
            return carry

        lax.fori_loop(0, count, step, 0)
        for h in range(heads):
            sums = total[h : h + 1, :]
            o_ref[0, h] = (acc[h] / sums).astype(o_ref.dtype)
            l_ref[0, h : h + 1, :] = peak[h : h + 1, :] + jnp.log(sums)


def wake_attention(every_query, table, places, counts, heads):
    blocks, _, width = every_query.shape
    return pl.pallas_call(
        functools.partial(wake_kernel, heads),
        grid_spec=pltpu.PrefetchScalarGridSpec(
            num_scalar_prefetch=2,
            grid=(blocks,),
            in_specs=[
                pl.BlockSpec((1, BLOCK, width), lambda b, i, c: (b, 0, 0)),
                pl.BlockSpec(table.shape, lambda b, i, c: (0, 0, 0)),
            ],
            out_specs=[
                pl.BlockSpec((1, heads, HEAD_DIM, BLOCK), lambda b, i, c: (b, 0, 0, 0)),
                pl.BlockSpec((1, heads, BLOCK), lambda b, i, c: (b, 0, 0)),
            ],
            scratch_shapes=[
                pltpu.VMEM((heads, HEAD_DIM, BLOCK), jnp.float32),
                pltpu.VMEM((heads, BLOCK), jnp.float32),
                pltpu.VMEM((heads, BLOCK), jnp.float32),
            ],
        ),
        out_shape=[
            jax.ShapeDtypeStruct((blocks, heads, HEAD_DIM, BLOCK), jnp.bfloat16),
            jax.ShapeDtypeStruct((blocks, heads, BLOCK), jnp.float32),
        ],
        compiler_params=pltpu.CompilerParams(vmem_limit_bytes=VMEM_BYTES),
        cost_estimate=pl.CostEstimate(
            flops=blocks * BLOCK * BLOCK * width * 4, bytes_accessed=blocks * BLOCK * width * 4, transcendentals=blocks * BLOCK * BLOCK * heads
        ),
    )(places, counts, every_query, table)


def final_kernel(heads, n_parts, *refs):
    out_ref = refs[-1]
    for h in range(heads):
        logs = [refs[2 * j + 1][0, h : h + 1, :] for j in range(n_parts)]
        peak = functools.reduce(jnp.maximum, logs)
        shares = [jnp.exp(one - peak) for one in logs]
        total = functools.reduce(jnp.add, shares)
        out = jnp.zeros((HEAD_DIM, BLOCK), jnp.float32)
        for j in range(n_parts):
            out += refs[2 * j][0, h].astype(jnp.float32) * (shares[j] / total)
        out_ref[:, head_cols(h)] = out.T.astype(out_ref.dtype)


def final_merge(parts, heads):
    blocks = parts[0][0].shape[0]
    flat, specs = [], []
    for values, logs in parts:
        flat += [values, logs]
        specs += [
            pl.BlockSpec((1, heads, HEAD_DIM, BLOCK), lambda b: (b, 0, 0, 0)),
            pl.BlockSpec((1, heads, BLOCK), lambda b: (b, 0, 0)),
        ]
    return pl.pallas_call(
        functools.partial(final_kernel, heads, len(parts)),
        grid=(blocks,),
        in_specs=specs,
        out_specs=pl.BlockSpec((BLOCK, heads * HEAD_DIM), lambda b: (b, 0)),
        out_shape=jax.ShapeDtypeStruct((blocks * BLOCK, heads * HEAD_DIM), jnp.bfloat16),
        compiler_params=pltpu.CompilerParams(vmem_limit_bytes=VMEM_BYTES),
    )(*flat)


def merge(first, second):
    (o1, l1), (o2, l2) = first, second
    peak = jnp.maximum(l1, l2)
    e1, e2 = jnp.exp(l1 - peak), jnp.exp(l2 - peak)
    total = e1 + e2
    w1, w2 = (e1 / total)[:, :, None, :], (e2 / total)[:, :, None, :]
    out = o1.astype(jnp.float32) * w1 + o2.astype(jnp.float32) * w2
    return out.astype(jnp.bfloat16), peak + jnp.log(total)


def send(part, pairs):
    return tuple(lax.ppermute(leaf, "tok", pairs) for leaf in part)


def live_if(part, flag):
    return part[0], jnp.where(flag, part[1], NEVER)


def return_parts(values, logs, lines):
    place = lax.axis_index("tok")
    z, y = place // 2, place % 2
    across = [(i, i ^ 1) for i in range(2 * lines)]

    def pick(z_to, y_to):
        at = z_to * 2 + y_to
        return tuple(lax.dynamic_index_in_dim(leaf, at, 0, keepdims=False) for leaf in (values, logs))

    ready = {}

    def joined(k):
        k = k % lines
        if k not in ready:
            z_to = (z + k) % lines
            ready[k] = merge(pick(z_to, y), send(pick(z_to, 1 - y), across))
        return ready[k]

    up = down = None
    for k in range(lines - 1, 0, -1):
        here_up, here_down = joined(k), joined(lines - k)
        if up is not None:
            here_up = merge(here_up, live_if(up, z >= 1))
            here_down = merge(here_down, live_if(down, z <= lines - 2))
        up_pairs = [(2 * i + j, 2 * i + 2 + j) for i in range(lines - k) for j in range(2)]
        down_pairs = [(2 * i + j, 2 * i - 2 + j) for i in range(k, lines) for j in range(2)]
        up, down = send(here_up, up_pairs), send(here_down, down_pairs)
    own = joined(0)
    return [own, live_if(up, z >= 1), live_if(down, z <= lines - 2)]


def on_device(
    tokens,
    norm_gain,
    w_query,
    w_key,
    w_value,
    w_out,
    kv_cache,
    wake_blocks,
    wake_frames,
    wake_counts,
):
    tok_rows = tokens.shape[0]
    local_width = w_query.shape[1]
    heads = local_width // HEAD_DIM
    blocks_dev = tok_rows // BLOCK
    tok_devices = lax.axis_size("tok")
    tok_place = lax.axis_index("tok")
    model_place = lax.axis_index("mp")
    tokens_f32 = tokens.astype(jnp.float32)
    inverse = lax.rsqrt(jnp.mean(tokens_f32 * tokens_f32, axis=1, keepdims=True) + 1e-05)
    normed = (tokens_f32 * inverse * norm_gain[None, :]).astype(jnp.bfloat16)
    queries = jnp.dot(normed, w_query, preferred_element_type=jnp.float32).astype(jnp.bfloat16)
    every_query = lax.all_gather(queries, "tok", axis=0, tiled=True)
    keys_now = jnp.dot(normed, w_key, preferred_element_type=jnp.float32).astype(jnp.bfloat16)
    values_now = jnp.dot(normed, w_value, preferred_element_type=jnp.float32).astype(jnp.bfloat16)
    forward = [(i, (i + 1) % tok_devices) for i in range(tok_devices)]
    backward = [(j, i) for i, j in forward]

    def with_halo(rows):
        low = lax.ppermute(rows[tok_rows - BLOCK :], "tok", forward)
        high = lax.ppermute(rows[:BLOCK], "tok", backward)
        return jnp.concatenate([low, rows, high], axis=0)

    near = near_attention(queries, with_halo(keys_now), with_halo(values_now), heads)

    live = jnp.arange(WMAX, dtype=jnp.int32)[None, :] < wake_counts[:, None]
    held = live & (wake_blocks // blocks_dev == tok_place)
    position = jnp.cumsum(held.astype(jnp.int32), axis=1) - 1
    local_index = wake_frames * blocks_dev + wake_blocks % blocks_dev
    picked = held[:, None, :] & (position[:, None, :] == jnp.arange(WMAX, dtype=jnp.int32)[None, :, None])
    places = jnp.sum(jnp.where(picked, local_index[:, None, :], 0), axis=2).reshape(-1)
    counts = jnp.sum(held.astype(jnp.int32), axis=1)
    table = kv_cache.reshape(kv_cache.shape[0] * blocks_dev, BLOCK, 2 * local_width)
    far_values, far_logs = wake_attention(
        every_query.reshape(-1, BLOCK, local_width), table, places, counts, heads
    )
    shape = (tok_devices, blocks_dev, heads)
    parts = return_parts(
        far_values.reshape(shape + (HEAD_DIM, BLOCK)), far_logs.reshape(shape + (BLOCK,)), tok_devices // 2
    )
    attention = final_merge([tuple(near)] + parts, heads)
    gathered = lax.all_gather(attention, "mp", axis=1, tiled=True)
    out_cols = lax.dynamic_slice_in_dim(w_out, model_place * local_width, local_width, 1)
    mixed = jnp.dot(gathered, out_cols, preferred_element_type=jnp.float32)
    residual_part = lax.dynamic_slice_in_dim(tokens, model_place * local_width, local_width, 1)
    return (residual_part.astype(jnp.float32) + mixed).astype(jnp.bfloat16)


def solution(mesh):
    return jax.shard_map(
        on_device,
        mesh=mesh,
        in_specs=(
            P("tok", None),
            P(),
            P(None, "mp"),
            P(None, "mp"),
            P(None, "mp"),
            P(),
            P(None, "tok", None, "mp"),
            P(),
            P(),
            P(),
        ),
        out_specs=P("tok", "mp"),
        check_vma=False,
    )
```

time: 620 us -> 427 us (0.69)
  waiting for transfers between devices: 409 us -> 242 us
  local copies, waits for them, and re-layouts: 91 us -> 15.3 us
  starting transfers between devices: 12.1 us -> 71.6 us
  Pallas kernels: 0 us -> 53.8 us
  matrix products: 47.7 us -> 14.6 us
  other arithmetic: 45.1 us -> 14.5 us
    ppermute x2 -> x24, waiting for transfers between devices: 257 us -> 88.3 us  [the longest x20 88.3 us: send(): return tuple((lax.ppermute(leaf, 'tok', pairs) for leaf in part))]
    all_gather x0 -> x2, waiting for transfers between devices: none -> 154 us  [the longest x1 120 us: on_device(): every_query = lax.all_gather(queries, 'tok', axis=0, tiled=True)]
    reduce_scatter x1 -> x0, waiting for transfers between devices: 86.8 us -> none  [on_device(): lax.psum_scatter(partial_sum, 'mp', scatter_dimension=1, tiled=True)]
    ppermute x2 -> x24, starting transfers between devices: 4.72 us -> 71.6 us  [the longest x20 65.8 us: send(): return tuple((lax.ppermute(leaf, 'tok', pairs) for leaf in part))]
    all_to_all x1 -> x0, waiting for transfers between devices: 64.8 us -> none  [on_device(): lax.all_to_all(outgoing, 'tok', split_axis=0, concat_axis=0, tiled=True)]
    pallas_call x0 -> x3, Pallas kernels: none -> 53.8 us  [the longest x1 45.3 us: wake_attention(): pl.pallas_call(functools.partial(wake_kernel, heads), grid_spec=pltpu.Pre...]
    slice x3 -> x2, local copies, waits for them, and re-layouts: 46.7 us -> 0.04 us  [with_halo(): low = lax.ppermute(rows[tok_rows - BLOCK:], 'tok', forward)]
    concatenate x3 -> x2, other arithmetic: 31 us -> 0.17 us  [with_halo(): return jnp.concatenate([low, rows, high], axis=0)]
  transfers between devices with their start and end apart: 4 -> 26, of which waited for: 3 -> 11; matrix products, arithmetic and copies ran while one was open for 7% -> 6% of each run, Pallas kernels for 0% -> 1%
where the time goes in v1:
time: 427 us; the launch traced here: 426 us
  waiting for transfers between devices  242 us (57%)
  starting transfers between devices  71.6 us (17%)
  Pallas kernels  53.8 us (13%)
  local copies, waits for them, and re-layouts  15.3 us (4%)
  matrix products  14.6 us (3%)
  other arithmetic  14.5 us (3%)
  between operations  14 us (3%)
    all_gather x1, waiting for transfers between devices, on_device(): every_query = lax.all_gather(queries, 'tok', axis=0, tiled=True)  120 us
    ppermute x20, waiting for transfers between devices, send(): return tuple((lax.ppermute(leaf, 'tok', pairs) for leaf in part))  88.3 us
    ppermute x20, starting transfers between devices, send(): return tuple((lax.ppermute(leaf, 'tok', pairs) for leaf in part))  65.8 us
    pallas_call x1, Pallas kernels, wake_attention(): pl.pallas_call(functools.partial(wake_kernel, heads), grid_spec=pltpu.Pre...  45.3 us
    all_gather x1, waiting for transfers between devices, on_device(): gathered = lax.all_gather(attention, 'mp', axis=1, tiled=True)  34.1 us
    convert_element_type x5, other arithmetic, merge(): return (out.astype(jnp.bfloat16), peak + jnp.log(total))  10.7 us
  transfers between devices with their start and end apart: 26, of which 11 were waited for; matrix products, arithmetic and copies ran while one was open for 6% of the time, Pallas kernels for 1%

profile of v1, /device:TPU:0, one launch (start us, length us, event | category | flops | bytes accessed | tf_op | source)
XLA Modules:
  0.0 425.8 jit_solution(10876071076743919486)
XLA Ops:
  6.5 3.2 fusion
  10.6 3.4 convolution_convert_fusion.2.q_ref
  14.5 7.8 %reshape.60.table_ref = bf16[16,128,1024]{2,1,0:T(8,128)(2,1)} reshape(bf16[2,1024,2,512]{3,2,1,0:T(2,128)(2,1)} %param.16) | data formatting | bytes 8388608 | tf_op jit(solution)/shard_map/reshape | solution.py:264
  22.2 119.6 %all-gather.3.cloned.1.call-done = bf16[8192,512]{1,0:T(8,128)(2,1)} async-done(((bf16[1024,512]{1,0:T(8,128)(2,1)}), bf16[8192,512]{1,0:T(8,128)(2,1)}) %all-gather.3.cloned.1.call-update) | async-done | bytes 8388624 | tf_op jit(solution)/shard_map/all_gather | solution.py:244
  141.8 2.2 copy-done.2
  144.0 45.3 %shard_map.101 = (bf16[64,4,128,128]{3,2,1,0:T(8,128)(2,1)S(1)}, f32[64,4,128]{2,1,0:T(4,128)S(1)}) custom-call(s32[512]{0:T(512)S(1)} %reshape.58.idx_ref, s32[64]{0:T(128)S(1)} %get-tuple-element.19.cnt_ref, bf16[64,128,512]{2,1,0:T(8,128)(2,1)} %bitcast.127, bf16[16,128,1024]{2,1,0:T(8,128)(2,1)S(1)} %copy-done.2), custom_call_target="tpu_custom_call" | custom-call | flops 2147483648 | bytes 16777216 | tf_op jit(solution)/shard_map/pallas_call | solution.py:110
  189.3 2.2 dynamic-slice_bitcast_fusion
  191.5 2.1 copy-done.3
  193.6 26.8 %collective-permute-start.7 = (bf16[8,4,128,128]{3,2,1,0:T(8,128)(2,1)S(1)}, bf16[8,4,128,128]{3,2,1,0:T(8,128)(2,1)}, u32[]{:S(2)}, u32[]{:S(2)}) collective-permute-start(bf16[8,4,128,128]{3,2,1,0:T(8,128)(2,1)S(1)} %get-tuple-element.25), channel_id=1, source_target_pairs={{0,4},{4,0},{8,12},{12,8},{16,20},{20,16},{24,28},{28,24},{1,5},{5... | collective-permute-start | bytes 3145736 | tf_op jit(solution)/shard_map/ppermute | solution.py:183
  222.5 22.4 %collective-permute-done.6 = f32[8,4,128]{2,1,0:T(4,128)S(1)} collective-permute-done((f32[8,4,128]{2,1,0:T(4,128)S(1)}, f32[8,4,128]{2,1,0:T(4,128)S(1)}, u32[]{:S(2)}, u32[]{:S(2)}) %collective-permute-start.6) | collective-permute-done | bytes 16416 | tf_op jit(solution)/shard_map/ppermute | solution.py:183
  244.9 2.1 fusion.12
  251.5 15.0 %collective-permute-done.8 = f32[8,4,128]{2,1,0:T(4,128)S(1)} collective-permute-done((f32[8,4,128]{2,1,0:T(4,128)S(1)}, f32[8,4,128]{2,1,0:T(4,128)S(1)}, u32[]{:S(2)}, u32[]{:S(2)}) %collective-permute-start.8) | collective-permute-done | bytes 16416 | tf_op jit(solution)/shard_map/ppermute | solution.py:183
  270.4 4.0 collective-permute-start.10
  275.9 2.6 fusion.6
  280.7 20.0 %collective-permute-done.13 = bf16[8,4,128,128]{3,2,1,0:T(8,128)(2,1)S(1)} collective-permute-done((bf16[8,4,128,128]{3,2,1,0:T(8,128)(2,1)}, bf16[8,4,128,128]{3,2,1,0:T(8,128)(2,1)S(1)}, u32[]{:S(2)}, u32[]{:S(2)}) %collective-permute-start.13) | collective-permute-done | bytes 1048608 | tf_op jit(solution)/shard_map/ppermute | solution.py:183
  300.7 2.4 add_convert_fusion.1
  303.1 3.9 collective-permute-start.14
  307.0 2.4 convolution_convert_fusion
  310.4 3.8 collective-permute-start.3
  314.2 8.0 %collective-permute-done.5 = bf16[8,4,128,128]{3,2,1,0:T(8,128)(2,1)S(1)} collective-permute-done((bf16[8,4,128,128]{3,2,1,0:T(8,128)(2,1)S(1)}, bf16[8,4,128,128]{3,2,1,0:T(8,128)(2,1)S(1)}, u32[]{:S(2)}, u32[]{:S(2)}) %collective-permute-start.5) | collective-permute-done | bytes 1048608 | tf_op jit(solution)/shard_map/ppermute | solution.py:183
  322.2 3.3 collective-permute-done.14
  325.5 3.1 fusion.4
  328.6 4.5 %collective-permute-start.15 = (bf16[8,4,128,128]{3,2,1,0:T(8,128)(2,1)S(1)}, bf16[8,4,128,128]{3,2,1,0:T(8,128)(2,1)S(1)}, u32[]{:S(2)}, u32[]{:S(2)}) collective-permute-start(bf16[8,4,128,128]{3,2,1,0:T(8,128)(2,1)S(1)} %get-tuple-element.21), channel_id=1, source_target_pairs={{0,8},{4,12},{8,16},{12,20},{1,9},{5,13},{9,17},{13,21},{2,10},{6,... | collective-permute-start | bytes 3145736 | tf_op jit(solution)/shard_map/ppermute | solution.py:183
  333.1 2.4 convolution_convert_fusion.1
  338.4 14.1 %collective-permute-done.11 = f32[8,4,128]{2,1,0:T(4,128)S(1)} collective-permute-done((f32[8,4,128]{2,1,0:T(4,128)S(1)}, f32[8,4,128]{2,1,0:T(4,128)S(1)}, u32[]{:S(2)}, u32[]{:S(2)}) %collective-permute-start.11) | collective-permute-done | bytes 16416 | tf_op jit(solution)/shard_map/ppermute | solution.py:183
  354.4 5.2 %collective-permute-start.16 = (bf16[8,4,128,128]{3,2,1,0:T(8,128)(2,1)S(1)}, bf16[8,4,128,128]{3,2,1,0:T(8,128)(2,1)S(1)}, u32[]{:S(2)}, u32[]{:S(2)}) collective-permute-start(bf16[8,4,128,128]{3,2,1,0:T(8,128)(2,1)S(1)} %add_convert_fusion.2), channel_id=1, source_target_pairs={{0,8},{4,12},{8,16},{12,20},{16,24},{20,28},{1,9},{5,13},{9,17},{1... | collective-permute-start | bytes 3145736 | tf_op jit(solution)/shard_map/ppermute | solution.py:183
  361.1 4.9 %shard_map.100 = (f32[8,4,128,128]{3,2,1,0:T(8,128)S(1)}, f32[8,4,128]{2,1,0:T(4,128)S(1)}) custom-call(bf16[1024,512]{1,0:T(8,128)(2,1)S(1)} %copy-done.4, bf16[1280,512]{1,0:T(8,128)(2,1)S(1)} %pad_maximum_fusion.k0.k1.k2, bf16[1280,512]{1,0:T(8,128)(2,1)S(1)} %pad_maximum_fusion.k0.k1.k2, bf16[1280,512]{1,0:T(8,128)(2,1)S(1)} %pad_maximum_fusion.k0.k1.k2, ...), custom_call_target="tpu_custom_call" | custom-call | flops 805306368 | bytes 10485760 | tf_op jit(solution)/shard_map/pallas_call | solution.py:50
  366.0 4.5 %collective-permute-start.17 = (f32[8,4,128]{2,1,0:T(4,128)S(1)}, f32[8,4,128]{2,1,0:T(4,128)S(1)}, u32[]{:S(2)}, u32[]{:S(2)}) collective-permute-start(f32[8,4,128]{2,1,0:T(4,128)S(1)} %get-tuple-element.48), channel_id=1, source_target_pairs={{0,8},{4,12},{8,16},{12,20},{16,24},{20,28},{1,9},{5,13},{9,17},{1... | collective-permute-start | bytes 49160 | tf_op jit(solution)/shard_map/ppermute | solution.py:183
  370.9 3.9 collective-permute-done.17
  374.8 3.6 shard_map.102
  378.4 34.1 %all-gather.5.cloned.1.call-done = bf16[1024,2048]{1,0:T(8,128)(2,1)} async-done(((bf16[1024,512]{1,0:T(8,128)(2,1)}), bf16[1024,2048]{1,0:T(8,128)(2,1)}) %all-gather.5.cloned.1.call-update) | async-done | bytes 4194320 | tf_op jit(solution)/shard_map/all_gather | solution.py:273
  412.5 6.5 %add_convert_fusion = bf16[1024,512]{1,0:T(8,128)(2,1)} fusion(bf16[1024,2048]{1,0:T(8,128)(2,1)} %all-gather.5.cloned.1.call-done, bf16[2048,2048]{1,0:T(8,128)(2,1)} %param.15, s32[]{:T(128)S(6)} %select_n.110, bf16[1024,2048]{1,0:T(8,128)(2,1)} %param.10), kind=kOutput, calls=%fused_computation.23 | convolution fusion | flops 2149056512 | bytes 8389632 | tf_op jit(solution)/shard_map/dot_general | solution.py:275
  (86 shorter events, 22.7 us)
Async XLA Ops:
  6.5 135.3 %all-gather.3.cloned.1.call-start = ((), (), s32[]{:S(2)}) async-start(), calls=%async_computation | async-start | bytes 9437184 | tf_op jit(solution)/shard_map/all_gather | solution.py:244
  14.0 398.5 %all-gather.5.cloned.1.call-start = ((), (), s32[]{:S(2)}) async-start(), calls=%async_computation.1 | async-start | bytes 5242880 | tf_op jit(solution)/shard_map/all_gather | solution.py:273
  189.3 4.3 %copy-start.3 = (bf16[64,4,128,128]{3,2,1,0:T(8,128)(2,1)}, bf16[64,4,128,128]{3,2,1,0:T(8,128)(2,1)S(1)}, u32[]{:S(2)}) copy-start(bf16[64,4,128,128]{3,2,1,0:T(8,128)(2,1)S(1)} %get-tuple-element.11) | copy-start | bytes 25165828
  193.6 51.3 %collective-permute-start.7 = (bf16[8,4,128,128]{3,2,1,0:T(8,128)(2,1)S(1)}, bf16[8,4,128,128]{3,2,1,0:T(8,128)(2,1)}, u32[]{:S(2)}, u32[]{:S(2)}) collective-permute-start(bf16[8,4,128,128]{3,2,1,0:T(8,128)(2,1)S(1)} %get-tuple-element.25), channel_id=1, source_target_pairs={{0,4},{4,0},{8,12},{12,8},{16,20},{20,16},{24,28},{28,24},{1,5},{5... | collective-permute-start | bytes 3145736 | tf_op jit(solution)/shard_map/ppermute | solution.py:183
  220.4 24.4 %collective-permute-start.6 = (f32[8,4,128]{2,1,0:T(4,128)S(1)}, f32[8,4,128]{2,1,0:T(4,128)S(1)}, u32[]{:S(2)}, u32[]{:S(2)}) collective-permute-start(f32[8,4,128]{2,1,0:T(4,128)S(1)} %get-tuple-element.46), channel_id=1, source_target_pairs={{0,4},{4,0},{8,12},{12,8},{16,20},{20,16},{24,28},{28,24},{1,5},{5... | collective-permute-start | bytes 49160 | tf_op jit(solution)/shard_map/ppermute | solution.py:183
  220.5 55.4 %collective-permute-start.12 = (bf16[8,4,128,128]{3,2,1,0:T(8,128)(2,1)}, bf16[8,4,128,128]{3,2,1,0:T(8,128)(2,1)S(1)}, u32[]{:S(2)}, u32[]{:S(2)}) collective-permute-start(bf16[8,4,128,128]{3,2,1,0:T(8,128)(2,1)} %get-tuple-element.24), channel_id=1, source_target_pairs={{0,4},{4,0},{8,12},{12,8},{16,20},{20,16},{24,28},{28,24},{1,5},{5... | collective-permute-start | bytes 3145736 | tf_op jit(solution)/shard_map/ppermute | solution.py:183
  247.0 28.9 %collective-permute-start.20 = (bf16[8,4,128,128]{3,2,1,0:T(8,128)(2,1)S(1)}, bf16[8,4,128,128]{3,2,1,0:T(8,128)(2,1)}, u32[]{:S(2)}, u32[]{:S(2)}) collective-permute-start(bf16[8,4,128,128]{3,2,1,0:T(8,128)(2,1)S(1)} %fusion.12), channel_id=1, source_target_pairs={{24,16},{28,20},{25,17},{29,21},{26,18},{30,22},{27,19},{31,23}} | collective-permute-start | bytes 3145736 | tf_op jit(solution)/shard_map/ppermute | solution.py:183
  248.7 17.8 %collective-permute-start.8 = (f32[8,4,128]{2,1,0:T(4,128)S(1)}, f32[8,4,128]{2,1,0:T(4,128)S(1)}, u32[]{:S(2)}, u32[]{:S(2)}) collective-permute-start(f32[8,4,128]{2,1,0:T(4,128)S(1)} %get-tuple-element.45), channel_id=1, source_target_pairs={{0,4},{4,0},{8,12},{12,8},{16,20},{20,16},{24,28},{28,24},{1,5},{5... | collective-permute-start | bytes 49160 | tf_op jit(solution)/shard_map/ppermute | solution.py:183
  250.8 17.5 %collective-permute-start.18 = (f32[8,4,128]{2,1,0:T(4,128)S(1)}, f32[8,4,128]{2,1,0:T(4,128)S(1)}, u32[]{:S(2)}, u32[]{:S(2)}) collective-permute-start(f32[8,4,128]{2,1,0:T(4,128)S(1)} %get-tuple-element.35), channel_id=1, source_target_pairs={{24,16},{28,20},{25,17},{29,21},{26,18},{30,22},{27,19},{31,23}} | collective-permute-start | bytes 49160 | tf_op jit(solution)/shard_map/ppermute | solution.py:183
  251.4 17.6 %collective-permute-start.4 = (f32[8,4,128]{2,1,0:T(4,128)S(1)}, f32[8,4,128]{2,1,0:T(4,128)S(1)}, u32[]{:S(2)}, u32[]{:S(2)}) collective-permute-start(f32[8,4,128]{2,1,0:T(4,128)S(1)} %get-tuple-element.47), channel_id=1, source_target_pairs={{0,4},{4,0},{8,12},{12,8},{16,20},{20,16},{24,28},{28,24},{1,5},{5... | collective-permute-start | bytes 49160 | tf_op jit(solution)/shard_map/ppermute | solution.py:183
  266.5 3.7 collective-permute-start.9
  268.3 1.9 collective-permute-start.19
  270.4 5.5 %collective-permute-start.10 = (f32[8,4,128]{2,1,0:T(4,128)S(1)}, f32[8,4,128]{2,1,0:T(4,128)S(1)}, u32[]{:S(2)}, u32[]{:S(2)}) collective-permute-start(f32[8,4,128]{2,1,0:T(4,128)S(1)} %get-tuple-element.14), channel_id=1, source_target_pairs={{0,8},{4,12},{1,9},{5,13},{2,10},{6,14},{3,11},{7,15}} | collective-permute-start | bytes 49160 | tf_op jit(solution)/shard_map/ppermute | solution.py:183
  274.3 26.4 %collective-permute-start.13 = (bf16[8,4,128,128]{3,2,1,0:T(8,128)(2,1)}, bf16[8,4,128,128]{3,2,1,0:T(8,128)(2,1)S(1)}, u32[]{:S(2)}, u32[]{:S(2)}) collective-permute-start(bf16[8,4,128,128]{3,2,1,0:T(8,128)(2,1)} %get-tuple-element.23), channel_id=1, source_target_pairs={{0,4},{4,0},{8,12},{12,8},{16,20},{20,16},{24,28},{28,24},{1,5},{5... | collective-permute-start | bytes 3145736 | tf_op jit(solution)/shard_map/ppermute | solution.py:183
  275.9 31.1 %copy-start.11 = (bf16[2048,512]{1,0:T(8,128)(2,1)S(1)}, bf16[2048,512]{1,0:T(8,128)(2,1)}, u32[]{:S(2)}) copy-start(bf16[2048,512]{1,0:T(8,128)(2,1)} %param.14) | copy-start | bytes 6291460
  278.5 22.2 %collective-permute-start.21 = (bf16[8,4,128,128]{3,2,1,0:T(8,128)(2,1)S(1)}, bf16[8,4,128,128]{3,2,1,0:T(8,128)(2,1)S(1)}, u32[]{:S(2)}, u32[]{:S(2)}) collective-permute-start(bf16[8,4,128,128]{3,2,1,0:T(8,128)(2,1)S(1)} %fusion.6), channel_id=1, source_target_pairs={{16,8},{20,12},{24,16},{28,20},{17,9},{21,13},{25,17},{29,21},{18,... | collective-permute-start | bytes 3145736 | tf_op jit(solution)/shard_map/ppermute | solution.py:183
  279.3 42.9 %collective-permute-start.5 = (bf16[8,4,128,128]{3,2,1,0:T(8,128)(2,1)S(1)}, bf16[8,4,128,128]{3,2,1,0:T(8,128)(2,1)S(1)}, u32[]{:S(2)}, u32[]{:S(2)}) collective-permute-start(bf16[8,4,128,128]{3,2,1,0:T(8,128)(2,1)S(1)} %copy-done.7), channel_id=1, source_target_pairs={{0,4},{4,0},{8,12},{12,8},{16,20},{20,16},{24,28},{28,24},{1,5},{5... | collective-permute-start | bytes 3145736 | tf_op jit(solution)/shard_map/ppermute | solution.py:183
  300.7 6.3 %copy-start.6 = (bf16[1024,2048]{1,0:T(8,128)(2,1)S(1)}, bf16[1024,2048]{1,0:T(8,128)(2,1)}, u32[]{:S(2)}) copy-start(bf16[1024,2048]{1,0:T(8,128)(2,1)} %param.10) | copy-start | bytes 12582916
  303.1 22.4 %collective-permute-start.14 = (bf16[8,4,128,128]{3,2,1,0:T(8,128)(2,1)S(1)}, bf16[8,4,128,128]{3,2,1,0:T(8,128)(2,1)S(1)}, u32[]{:S(2)}, u32[]{:S(2)}) collective-permute-start(bf16[8,4,128,128]{3,2,1,0:T(8,128)(2,1)S(1)} %get-tuple-element.16), channel_id=1, source_target_pairs={{0,8},{4,12},{1,9},{5,13},{2,10},{6,14},{3,11},{7,15}} | collective-permute-start | bytes 3145736 | tf_op jit(solution)/shard_map/ppermute | solution.py:183
  309.4 45.0 %collective-permute-start.2 = (bf16[128,512]{1,0:T(8,128)(2,1)S(1)}, bf16[128,512]{1,0:T(8,128)(2,1)S(1)}, u32[]{:S(2)}, u32[]{:S(2)}) collective-permute-start(bf16[128,512]{1,0:T(8,128)(2,1)S(1)} %get-tuple-element.27), channel_id=1, source_target_pairs={{0,4},{4,8},{8,12},{12,16},{16,20},{20,24},{24,28},{28,0},{1,5},{5... | collective-permute-start | bytes 393224 | tf_op jit(solution)/shard_map/ppermute | solution.py:251
  310.4 49.2 %collective-permute-start.3 = (bf16[128,512]{1,0:T(8,128)(2,1)S(1)}, bf16[128,512]{1,0:T(8,128)(2,1)S(1)}, u32[]{:S(2)}, u32[]{:S(2)}) collective-permute-start(bf16[128,512]{1,0:T(8,128)(2,1)S(1)} %get-tuple-element.28), channel_id=1, source_target_pairs={{4,0},{8,4},{12,8},{16,12},{20,16},{24,20},{28,24},{0,28},{5,1},{9... | collective-permute-start | bytes 393224 | tf_op jit(solution)/shard_map/ppermute | solution.py:252
  325.5 7.6 %copy-start.12 = (bf16[2048,512]{1,0:T(8,128)(2,1)S(1)}, bf16[2048,512]{1,0:T(8,128)(2,1)}, u32[]{:S(2)}) copy-start(bf16[2048,512]{1,0:T(8,128)(2,1)} %param.13) | copy-start | bytes 6291460
  328.6 23.9 %collective-permute-start.15 = (bf16[8,4,128,128]{3,2,1,0:T(8,128)(2,1)S(1)}, bf16[8,4,128,128]{3,2,1,0:T(8,128)(2,1)S(1)}, u32[]{:S(2)}, u32[]{:S(2)}) collective-permute-start(bf16[8,4,128,128]{3,2,1,0:T(8,128)(2,1)S(1)} %get-tuple-element.21), channel_id=1, source_target_pairs={{0,8},{4,12},{8,16},{12,20},{1,9},{5,13},{9,17},{13,21},{2,10},{6,... | collective-permute-start | bytes 3145736 | tf_op jit(solution)/shard_map/ppermute | solution.py:183
  335.5 17.0 %collective-permute-start.11 = (f32[8,4,128]{2,1,0:T(4,128)S(1)}, f32[8,4,128]{2,1,0:T(4,128)S(1)}, u32[]{:S(2)}, u32[]{:S(2)}) collective-permute-start(f32[8,4,128]{2,1,0:T(4,128)S(1)} %get-tuple-element.51), channel_id=1, source_target_pairs={{0,8},{4,12},{8,16},{12,20},{1,9},{5,13},{9,17},{13,21},{2,10},{6,... | collective-permute-start | bytes 49160 | tf_op jit(solution)/shard_map/ppermute | solution.py:183
  337.4 22.3 %collective-permute-start = (bf16[128,512]{1,0:T(8,128)(2,1)S(1)}, bf16[128,512]{1,0:T(8,128)(2,1)S(1)}, u32[]{:S(2)}, u32[]{:S(2)}) collective-permute-start(bf16[128,512]{1,0:T(8,128)(2,1)S(1)} %get-tuple-element.29), channel_id=1, source_target_pairs={{0,4},{4,8},{8,12},{12,16},{16,20},{20,24},{24,28},{28,0},{1,5},{5... | collective-permute-start | bytes 393224 | tf_op jit(solution)/shard_map/ppermute | solution.py:251
  352.5 7.2 %collective-permute-start.1 = (bf16[128,512]{1,0:T(8,128)(2,1)S(1)}, bf16[128,512]{1,0:T(8,128)(2,1)S(1)}, u32[]{:S(2)}, u32[]{:S(2)}) collective-permute-start(bf16[128,512]{1,0:T(8,128)(2,1)S(1)} %get-tuple-element.30), channel_id=1, source_target_pairs={{4,0},{8,4},{12,8},{16,12},{20,16},{24,20},{28,24},{0,28},{5,1},{9... | collective-permute-start | bytes 393224 | tf_op jit(solution)/shard_map/ppermute | solution.py:252
  352.5 22.2 %collective-permute-start.22 = (bf16[8,4,128,128]{3,2,1,0:T(8,128)(2,1)S(1)}, bf16[8,4,128,128]{3,2,1,0:T(8,128)(2,1)S(1)}, u32[]{:S(2)}, u32[]{:S(2)}) collective-permute-start(bf16[8,4,128,128]{3,2,1,0:T(8,128)(2,1)S(1)} %get-tuple-element.15), channel_id=1, source_target_pairs={{8,0},{12,4},{16,8},{20,12},{24,16},{28,20},{9,1},{13,5},{17,9},{2... | collective-permute-start | bytes 3145736 | tf_op jit(solution)/shard_map/ppermute | solution.py:183
  354.3 6.8 %copy-start.4 = (bf16[1024,512]{1,0:T(8,128)(2,1)S(1)}, bf16[1024,512]{1,0:T(8,128)(2,1)}, u32[]{:S(2)}) copy-start(bf16[1024,512]{1,0:T(8,128)(2,1)} %convolution_convert_fusion.2.q_ref) | copy-start | bytes 3145732
  354.4 20.4 %collective-permute-start.16 = (bf16[8,4,128,128]{3,2,1,0:T(8,128)(2,1)S(1)}, bf16[8,4,128,128]{3,2,1,0:T(8,128)(2,1)S(1)}, u32[]{:S(2)}, u32[]{:S(2)}) collective-permute-start(bf16[8,4,128,128]{3,2,1,0:T(8,128)(2,1)S(1)} %add_convert_fusion.2), channel_id=1, source_target_pairs={{0,8},{4,12},{8,16},{12,20},{16,24},{20,28},{1,9},{5,13},{9,17},{1... | collective-permute-start | bytes 3145736 | tf_op jit(solution)/shard_map/ppermute | solution.py:183
  359.8 11.0 %collective-permute-start.23 = (f32[8,4,128]{2,1,0:T(4,128)S(1)}, f32[8,4,128]{2,1,0:T(4,128)S(1)}, u32[]{:S(2)}, u32[]{:S(2)}) collective-permute-start(f32[8,4,128]{2,1,0:T(4,128)S(1)} %get-tuple-element.13), channel_id=1, source_target_pairs={{8,0},{12,4},{16,8},{20,12},{24,16},{28,20},{9,1},{13,5},{17,9},{2... | collective-permute-start | bytes 49160 | tf_op jit(solution)/shard_map/ppermute | solution.py:183
  366.0 8.7 %collective-permute-start.17 = (f32[8,4,128]{2,1,0:T(4,128)S(1)}, f32[8,4,128]{2,1,0:T(4,128)S(1)}, u32[]{:S(2)}, u32[]{:S(2)}) collective-permute-start(f32[8,4,128]{2,1,0:T(4,128)S(1)} %get-tuple-element.48), channel_id=1, source_target_pairs={{0,8},{4,12},{8,16},{12,20},{16,24},{20,28},{1,9},{5,13},{9,17},{1... | collective-permute-start | bytes 49160 | tf_op jit(solution)/shard_map/ppermute | solution.py:183
  412.5 6.5 %copy-start.1 = (bf16[2048,512]{1,0:T(8,128)(2,1)S(1)}, bf16[2048,512]{1,0:T(8,128)(2,1)}, u32[]{:S(2)}) copy-start(bf16[2048,512]{1,0:T(8,128)(2,1)} %param.12) | copy-start | bytes 6291460
  (8 other events, 26.8 us)
Sparse Core Ops, SparseCore 0:
  14.1 127.6 all-gather.2
  378.5 33.9 all-gather.4

commit v2 on v1

--- a/solution.py
+++ b/solution.py
@@ -105,8 +105,8 @@
             l_ref[0, h : h + 1, :] = peak[h : h + 1, :] + jnp.log(sums)
 
 
-def wake_attention(every_query, table, places, counts, heads):
-    blocks, _, width = every_query.shape
+def wake_attention(some_query, table, places, counts, heads):
+    blocks, _, width = some_query.shape
     return pl.pallas_call(
         functools.partial(wake_kernel, heads),
         grid_spec=pltpu.PrefetchScalarGridSpec(
@@ -132,9 +132,9 @@
         ],
         compiler_params=pltpu.CompilerParams(vmem_limit_bytes=VMEM_BYTES),
         cost_estimate=pl.CostEstimate(
-            flops=blocks * BLOCK * BLOCK * width * 4, bytes_accessed=blocks * BLOCK * width * 4, transcendentals=blocks * BLOCK * BLOCK * heads
+            flops=blocks * BLOCK * BLOCK * width * 4, bytes_accessed=blocks * BLOCK * width * 32, transcendentals=blocks * BLOCK * BLOCK * heads
         ),
-    )(places, counts, every_query, table)
+    )(places, counts, some_query, table)
 
 
 def final_kernel(heads, n_parts, *refs):
@@ -187,35 +187,110 @@
     return part[0], jnp.where(flag, part[1], NEVER)
 
 
-def return_parts(values, logs, lines):
+def up_pairs(lines, hops):
+    return [(2 * i + j, 2 * i + 2 + j) for i in range(hops - 1, lines - 1) for j in range(2)]
+
+
+def down_pairs(lines, hops):
+    return [(2 * i + j, 2 * i - 2 + j) for i in range(1, lines + 1 - hops) for j in range(2)]
+
+
+def arrivals(lines):
+    table = []
+    for z in range(lines):
+        order = sorted((i for i in range(lines) if i != z), key=lambda i: (abs(i - z), (i + z) % 2 == 0, i))
+        table.append([z] + order)
+    return table
+
+
+def gather_queries(queries, lines):
+    place = lax.axis_index("tok")
+    z = place // 2
+    across = [(i, i ^ 1) for i in range(2 * lines)]
+    ups, downs = [queries], [queries]
+    others = [lax.ppermute(queries, "tok", across)]
+    for hops in range(1, lines):
+        ups.append(lax.ppermute(ups[-1], "tok", up_pairs(lines, hops)))
+        downs.append(lax.ppermute(downs[-1], "tok", down_pairs(lines, hops)))
+    mine = [queries]
+    table = arrivals(lines)
+    pieces = {}
+    for hops in range(1, lines):
+        pieces[hops], pieces[-hops] = ups[hops], downs[hops]
+    for j in range(1, lines):
+        chosen, used = None, []
+        for row in range(lines):
+            hops = row - table[row][j]
+            piece = pieces[hops]
+            used.append(hops)
+            chosen = piece if chosen is None else jnp.where(z == row, piece, chosen)
+        used = sorted(set(used))
+        chosen, *after = lax.optimization_barrier([chosen] + [pieces[hops] for hops in used])
+        pieces.update(zip(used, after))
+        mine.append(chosen)
+        others.append(lax.ppermute(chosen, "tok", across))
+    return mine, others
+
+
+def return_parts(get_part, lines):
     place = lax.axis_index("tok")
     z, y = place // 2, place % 2
     across = [(i, i ^ 1) for i in range(2 * lines)]
-
-    def pick(z_to, y_to):
-        at = z_to * 2 + y_to
-        return tuple(lax.dynamic_index_in_dim(leaf, at, 0, keepdims=False) for leaf in (values, logs))
-
-    ready = {}
-
-    def joined(k):
-        k = k % lines
-        if k not in ready:
-            z_to = (z + k) % lines
-            ready[k] = merge(pick(z_to, y), send(pick(z_to, 1 - y), across))
-        return ready[k]
+    table = arrivals(lines)
+    slots = []
+    for j in range(lines):
+        z_to = lookup([table[row][j] for row in range(lines)], z)
+        away = send(get_part(j, z_to * 2 + 1 - y, True), across)
+        slots.append(merge(get_part(j, z_to * 2 + y, False), away))
+
+    def joined(shift):
+        chosen = None
+        for row in range(lines):
+            piece = slots[table[row].index((row + shift) % lines)]
+            if chosen is None:
+                chosen = piece
+            else:
+                chosen = tuple(jnp.where(z == row, p, c) for p, c in zip(piece, chosen))
+        return chosen
 
     up = down = None
     for k in range(lines - 1, 0, -1):
-        here_up, here_down = joined(k), joined(lines - k)
+        here_up, here_down = joined(k), joined(-k)
         if up is not None:
             here_up = merge(here_up, live_if(up, z >= 1))
             here_down = merge(here_down, live_if(down, z <= lines - 2))
-        up_pairs = [(2 * i + j, 2 * i + 2 + j) for i in range(lines - k) for j in range(2)]
-        down_pairs = [(2 * i + j, 2 * i - 2 + j) for i in range(k, lines) for j in range(2)]
-        up, down = send(here_up, up_pairs), send(here_down, down_pairs)
-    own = joined(0)
-    return [own, live_if(up, z >= 1), live_if(down, z <= lines - 2)]
+        go_up = [(2 * i + j, 2 * i + 2 + j) for i in range(lines - k) for j in range(2)]
+        go_down = [(2 * i + j, 2 * i - 2 + j) for i in range(k, lines) for j in range(2)]
+        up, down = send(here_up, go_up), send(here_down, go_down)
+    return [slots[0], live_if(up, z >= 1), live_if(down, z <= lines - 2)]
+
+
+def lookup(values, at):
+    out = jnp.int32(values[0])
+    for i, value in enumerate(values):
+        out = jnp.where(at == i, jnp.int32(value), out)
+    return out
+
+
+def project_out(attention, out_cols):
+    width = attention.shape[1]
+    count = lax.axis_size("mp")
+    if count != 4:
+        gathered = lax.all_gather(attention, "mp", axis=1, tiled=True)
+        return jnp.dot(gathered, out_cols, preferred_element_type=jnp.float32)
+    place = lax.axis_index("mp")
+
+    def swap(piece, bit):
+        return lax.ppermute(piece, "mp", [(i, i ^ bit) for i in range(count)])
+
+    def product(piece, source):
+        rows = lax.dynamic_slice_in_dim(out_cols, source * width, width, 0)
+        return jnp.dot(piece, rows, preferred_element_type=jnp.float32)
+
+    far, near = swap(attention, 2), swap(attention, 1)
+    last = swap(far, 1)
+    total = product(attention, place) + product(near, place ^ 1)
+    return total + product(far, place ^ 2) + product(last, place ^ 3)
 
 
 def on_device(
@@ -241,7 +316,7 @@
     inverse = lax.rsqrt(jnp.mean(tokens_f32 * tokens_f32, axis=1, keepdims=True) + 1e-05)
     normed = (tokens_f32 * inverse * norm_gain[None, :]).astype(jnp.bfloat16)
     queries = jnp.dot(normed, w_query, preferred_element_type=jnp.float32).astype(jnp.bfloat16)
-    every_query = lax.all_gather(queries, "tok", axis=0, tiled=True)
+    mine, others = gather_queries(queries, tok_devices // 2)
     keys_now = jnp.dot(normed, w_key, preferred_element_type=jnp.float32).astype(jnp.bfloat16)
     values_now = jnp.dot(normed, w_value, preferred_element_type=jnp.float32).astype(jnp.bfloat16)
     forward = [(i, (i + 1) % tok_devices) for i in range(tok_devices)]
@@ -262,17 +337,22 @@
     places = jnp.sum(jnp.where(picked, local_index[:, None, :], 0), axis=2).reshape(-1)
     counts = jnp.sum(held.astype(jnp.int32), axis=1)
     table = kv_cache.reshape(kv_cache.shape[0] * blocks_dev, BLOCK, 2 * local_width)
-    far_values, far_logs = wake_attention(
-        every_query.reshape(-1, BLOCK, local_width), table, places, counts, heads
-    )
-    shape = (tok_devices, blocks_dev, heads)
-    parts = return_parts(
-        far_values.reshape(shape + (HEAD_DIM, BLOCK)), far_logs.reshape(shape + (BLOCK,)), tok_devices // 2
-    )
+    places, counts = places.reshape(tok_devices, -1), counts.reshape(tok_devices, -1)
+
+    def get_part(slot, reader, other):
+        piece = (others if other else mine)[slot].reshape(blocks_dev, BLOCK, local_width)
+        return wake_attention(
+            piece,
+            table,
+            lax.dynamic_index_in_dim(places, reader, 0, keepdims=False),
+            lax.dynamic_index_in_dim(counts, reader, 0, keepdims=False),
+            heads,
+        )
+
+    parts = return_parts(get_part, tok_devices // 2)
     attention = final_merge([tuple(near)] + parts, heads)
-    gathered = lax.all_gather(attention, "mp", axis=1, tiled=True)
     out_cols = lax.dynamic_slice_in_dim(w_out, model_place * local_width, local_width, 1)
-    mixed = jnp.dot(gathered, out_cols, preferred_element_type=jnp.float32)
+    mixed = project_out(attention, out_cols)
     residual_part = lax.dynamic_slice_in_dim(tokens, model_place * local_width, local_width, 1)
     return (residual_part.astype(jnp.float32) + mixed).astype(jnp.bfloat16)
 

time: 427 us -> 382 us (0.89)
  waiting for transfers between devices: 242 us -> 156 us
  starting transfers between devices: 71.6 us -> 123 us
  between operations: 14 us -> 0.76 us
  other arithmetic: 14.5 us -> 23.1 us
  Pallas kernels: 53.8 us -> 46.8 us
    all_gather x2 -> x0, waiting for transfers between devices: 154 us -> none  [the longest x1 120 us: on_device(): every_query = lax.all_gather(queries, 'tok', axis=0, tiled=True)]
    ppermute x0 -> x13, waiting for transfers between devices: none -> 90.9 us  [the longest x3 61.9 us: gather_queries(): downs.append(lax.ppermute(downs[-1], 'tok', down_pairs(lines, hops)))]
    ppermute x0 -> x13, starting transfers between devices: none -> 24.3 us  [the longest x3 8.93 us: gather_queries(): ups.append(lax.ppermute(ups[-1], 'tok', up_pairs(lines, hops)))]
    ppermute x20, waiting for transfers between devices: 88.3 us -> 64.9 us  [send(): return tuple((lax.ppermute(leaf, 'tok', pairs) for leaf in part))]
    ppermute x20, starting transfers between devices: 65.8 us -> 84.7 us  [send(): return tuple((lax.ppermute(leaf, 'tok', pairs) for leaf in part))]
    ppermute x2, starting transfers between devices: 1.92 us -> 13.8 us  [with_halo(): low = lax.ppermute(rows[tok_rows - BLOCK:], 'tok', forward)]
    select_n x0 -> x5, other arithmetic: none -> 10.8 us  [the longest x3 5.46 us: gather_queries(): chosen = piece if chosen is None else jnp.where(z == row, piece, chosen)]
    pallas_call x1 -> x8, Pallas kernels: 45.3 us -> 40.3 us  [wake_attention(): pl.pallas_call(functools.partial(wake_kernel, heads), grid_spec=pltpu.Pre...]
  transfers between devices with their start and end apart: 26 -> 37, of which waited for: 11 -> 10; matrix products, arithmetic and copies ran while one was open for 6% -> 8% of each run, Pallas kernels for 1% -> 12%
where the time goes in v2:
time: 382 us; the launch traced here: 380 us
  waiting for transfers between devices  156 us (41%)
  starting transfers between devices  123 us (32%)
  Pallas kernels  46.8 us (12%)
  other arithmetic  23.1 us (6%)
  matrix products  16.9 us (4%)
  local copies, waits for them, and re-layouts  14.1 us (4%)
    ppermute x20, starting transfers between devices, send(): return tuple((lax.ppermute(leaf, 'tok', pairs) for leaf in part))  84.7 us
    ppermute x20, waiting for transfers between devices, send(): return tuple((lax.ppermute(leaf, 'tok', pairs) for leaf in part))  64.9 us
    ppermute x3, waiting for transfers between devices, gather_queries(): downs.append(lax.ppermute(downs[-1], 'tok', down_pairs(lines, hops)))  61.9 us
    pallas_call x8, Pallas kernels, wake_attention(): pl.pallas_call(functools.partial(wake_kernel, heads), grid_spec=pltpu.Pre...  40.3 us
    ppermute x3, waiting for transfers between devices, gather_queries(): others.append(lax.ppermute(chosen, 'tok', across))  15.5 us
    ppermute x2, starting transfers between devices, with_halo(): low = lax.ppermute(rows[tok_rows - BLOCK:], 'tok', forward)  13.8 us
    ppermute x3, waiting for transfers between devices, swap(): return lax.ppermute(piece, 'mp', [(i, i ^ bit) for i in range(count)])  13.4 us
    dot_general x4, matrix products, product(): return jnp.dot(piece, rows, preferred_element_type=jnp.float32)  9.79 us
  transfers between devices with their start and end apart: 37, of which 10 were waited for; matrix products, arithmetic and copies ran while one was open for 8% of the time, Pallas kernels for 12%

profile of v2, /device:TPU:0, one launch (start us, length us, event | category | flops | bytes accessed | tf_op | source)
XLA Modules:
  0.0 380.4 jit_solution(14920280562831914448)
XLA Ops:
  0.0 3.2 fusion
  7.8 5.6 %collective-permute-start.7 = (bf16[1024,512]{1,0:T(8,128)(2,1)S(1)}, bf16[1024,512]{1,0:T(8,128)(2,1)S(1)}, u32[]{:S(2)}, u32[]{:S(2)}) collective-permute-start(bf16[1024,512]{1,0:T(8,128)(2,1)S(1)} %convolution_convert_fusion.2.q_ref), channel_id=1, source_target_pairs={{0,8},{4,12},{8,16},{12,20},{16,24},{20,28},{1,9},{5,13},{9,17},{1... | collective-permute-start | bytes 3145736 | tf_op jit(solution)/shard_map/ppermute | solution.py:213
  13.4 21.2 %collective-permute-done.10 = bf16[1024,512]{1,0:T(8,128)(2,1)S(1)} collective-permute-done((bf16[1024,512]{1,0:T(8,128)(2,1)S(1)}, bf16[1024,512]{1,0:T(8,128)(2,1)S(1)}, u32[]{:S(2)}, u32[]{:S(2)}) %collective-permute-start.10) | collective-permute-done | bytes 1048608 | tf_op jit(solution)/shard_map/ppermute | solution.py:214
  37.5 23.4 %collective-permute-done.11 = bf16[1024,512]{1,0:T(8,128)(2,1)} collective-permute-done((bf16[1024,512]{1,0:T(8,128)(2,1)S(1)}, bf16[1024,512]{1,0:T(8,128)(2,1)}, u32[]{:S(2)}, u32[]{:S(2)}) %collective-permute-start.11) | collective-permute-done | bytes 1048608 | tf_op jit(solution)/shard_map/ppermute | solution.py:214
  69.1 17.4 %collective-permute-done.12 = bf16[1024,512]{1,0:T(8,128)(2,1)} collective-permute-done((bf16[1024,512]{1,0:T(8,128)(2,1)}, bf16[1024,512]{1,0:T(8,128)(2,1)}, u32[]{:S(2)}, u32[]{:S(2)}) %collective-permute-start.12) | collective-permute-done | bytes 1048608 | tf_op jit(solution)/shard_map/ppermute | solution.py:214
  86.5 2.4 select_select_fusion.5
  90.3 7.7 %reshape.67.table_ref = bf16[16,128,1024]{2,1,0:T(8,128)(2,1)} reshape(bf16[2,1024,2,512]{3,2,1,0:T(2,128)(2,1)} %param.16) | data formatting | bytes 8388608 | tf_op jit(solution)/shard_map/reshape | solution.py:339
  100.3 5.7 %shard_map.108 = (bf16[8,4,128,128]{3,2,1,0:T(8,128)(2,1)}, f32[8,4,128]{2,1,0:T(4,128)S(1)}) custom-call(s32[64]{0:T(128)S(1)} %get-tuple-element.98.idx_ref, s32[8]{0:T(128)S(1)} %get-tuple-element.90.cnt_ref, bf16[8,128,512]{2,1,0:T(8,128)(2,1)} %bitcast.23.q_ref, bf16[16,128,1024]{2,1,0:T(8,128)(2,1)S(1)} %copy-done.2), custom_call_target="tpu_custom_call" | custom-call | flops 268435456 | bytes 16777216 | tf_op jit(solution)/shard_map/pallas_call | solution.py:110
  106.0 7.7 %collective-permute-start.21 = (bf16[8,4,128,128]{3,2,1,0:T(8,128)(2,1)}, bf16[8,4,128,128]{3,2,1,0:T(8,128)(2,1)}, u32[]{:S(2)}, u32[]{:S(2)}) collective-permute-start(bf16[8,4,128,128]{3,2,1,0:T(8,128)(2,1)} %get-tuple-element.52), channel_id=1, source_target_pairs={{0,4},{4,0},{8,12},{12,8},{16,20},{20,16},{24,28},{28,24},{1,5},{5... | collective-permute-start | bytes 3145736 | tf_op jit(solution)/shard_map/ppermute | solution.py:183
  113.9 5.8 %shard_map.106 = (bf16[8,4,128,128]{3,2,1,0:T(8,128)(2,1)}, f32[8,4,128]{2,1,0:T(4,128)S(1)}) custom-call(s32[64]{0:T(128)S(1)} %get-tuple-element.100.idx_ref, s32[8]{0:T(128)S(1)} %get-tuple-element.92.cnt_ref, bf16[8,128,512]{2,1,0:T(8,128)(2,1)} %bitcast.17.q_ref, bf16[16,128,1024]{2,1,0:T(8,128)(2,1)S(1)} %copy-done.2), custom_call_target="tpu_custom_call" | custom-call | flops 268435456 | bytes 16777216 | tf_op jit(solution)/shard_map/pallas_call | solution.py:110
  121.1 15.4 %collective-permute-done.13 = bf16[1024,512]{1,0:T(8,128)(2,1)} collective-permute-done((bf16[1024,512]{1,0:T(8,128)(2,1)}, bf16[1024,512]{1,0:T(8,128)(2,1)}, u32[]{:S(2)}, u32[]{:S(2)}) %collective-permute-start.13) | collective-permute-done | bytes 1048608 | tf_op jit(solution)/shard_map/ppermute | solution.py:231
  136.4 5.7 %shard_map.104 = (bf16[8,4,128,128]{3,2,1,0:T(8,128)(2,1)}, f32[8,4,128]{2,1,0:T(4,128)S(1)}) custom-call(s32[64]{0:T(128)S(1)} %get-tuple-element.97.idx_ref, s32[8]{0:T(128)S(1)} %get-tuple-element.89.cnt_ref, bf16[8,128,512]{2,1,0:T(8,128)(2,1)} %bitcast.11.q_ref, bf16[16,128,1024]{2,1,0:T(8,128)(2,1)S(1)} %copy-done.2), custom_call_target="tpu_custom_call" | custom-call | flops 268435456 | bytes 16777216 | tf_op jit(solution)/shard_map/pallas_call | solution.py:110
  148.3 53.2 %collective-permute-done.20 = f32[8,4,128]{2,1,0:T(4,128)S(1)} collective-permute-done((f32[8,4,128]{2,1,0:T(4,128)S(1)}, f32[8,4,128]{2,1,0:T(4,128)S(1)}, u32[]{:S(2)}, u32[]{:S(2)}) %collective-permute-start.20) | collective-permute-done | bytes 16416 | tf_op jit(solution)/shard_map/ppermute | solution.py:183
  202.8 4.4 %shard_map.103 = (bf16[8,4,128,128]{3,2,1,0:T(8,128)(2,1)S(1)}, f32[8,4,128]{2,1,0:T(4,128)S(1)}) custom-call(s32[64]{0:T(128)S(1)} %get-tuple-element.102.idx_ref, s32[8]{0:T(128)S(1)} %get-tuple-element.94.cnt_ref, bf16[8,128,512]{2,1,0:T(8,128)(2,1)} %bitcast.8.q_ref, bf16[16,128,1024]{2,1,0:T(8,128)(2,1)S(1)} %copy-done.2), custom_call_target="tpu_custom_call" | custom-call | flops 268435456 | bytes 16777216 | tf_op jit(solution)/shard_map/pallas_call | solution.py:110
  209.8 5.3 %fusion.9 = (bf16[8,4,128,128]{3,2,1,0:T(8,128)(2,1)}, bf16[8,4,128,128]{3,2,1,0:T(8,128)(2,1)}, bf16[8,4,128,128]{3,2,1,0:T(8,128)(2,1)}) fusion(pred[]{:T(512)S(6)} %eq.27, pred[]{:T(512)S(6)} %eq.26, pred[]{:T(512)S(6)} %eq.25, f32[8,4,128]{2,1,0:T(4,128)S(1)} %get-tuple-element.77, bf16[8,4,128,128]{3,2,1,0:T(8,128)(2,1)} %collective-permute-done.21, ...), kind=kLoop, calls=%fused_computation.30 | loop fusion | flops 11010048 | bytes 9535491 | tf_op jit(solution)/shard_map/jit(_where)/select_n | solution.py:253
  215.8 16.9 %collective-permute-start.22 = (f32[8,4,128]{2,1,0:T(4,128)S(1)}, f32[8,4,128]{2,1,0:T(4,128)S(1)}, u32[]{:S(2)}, u32[]{:S(2)}) collective-permute-start(f32[8,4,128]{2,1,0:T(4,128)S(1)} %get-tuple-element.54), channel_id=1, source_target_pairs={{0,8},{4,12},{1,9},{5,13},{2,10},{6,14},{3,11},{7,15}} | collective-permute-start | bytes 49160 | tf_op jit(solution)/shard_map/ppermute | solution.py:183
  235.3 2.8 fusion.6
  239.0 6.9 %collective-permute-start.4 = (bf16[1024,512]{1,0:T(8,128)(2,1)S(1)}, bf16[1024,512]{1,0:T(8,128)(2,1)S(1)}, u32[]{:S(2)}, u32[]{:S(2)}) collective-permute-start(bf16[1024,512]{1,0:T(8,128)(2,1)S(1)} %convolution_convert_fusion.2.q_ref), channel_id=1, source_target_pairs={{0,4},{4,0},{8,12},{12,8},{16,20},{20,16},{24,28},{28,24},{1,5},{5... | collective-permute-start | bytes 3145736 | tf_op jit(solution)/shard_map/ppermute | solution.py:211
  245.9 2.7 add_convert_fusion.1
  248.7 31.2 %collective-permute-start.24 = (bf16[8,4,128,128]{3,2,1,0:T(8,128)(2,1)S(1)}, bf16[8,4,128,128]{3,2,1,0:T(8,128)(2,1)S(1)}, u32[]{:S(2)}, u32[]{:S(2)}) collective-permute-start(bf16[8,4,128,128]{3,2,1,0:T(8,128)(2,1)S(1)} %get-tuple-element.56), channel_id=1, source_target_pairs={{0,8},{4,12},{1,9},{5,13},{2,10},{6,14},{3,11},{7,15}} | collective-permute-start | bytes 3145736 | tf_op jit(solution)/shard_map/ppermute | solution.py:183
  279.9 2.4 convolution_convert_fusion
  282.3 6.9 %collective-permute-start.2 = (bf16[128,512]{1,0:T(8,128)(2,1)S(1)}, bf16[128,512]{1,0:T(8,128)(2,1)S(1)}, u32[]{:S(2)}, u32[]{:S(2)}) collective-permute-start(bf16[128,512]{1,0:T(8,128)(2,1)S(1)} %get-tuple-element.64), channel_id=1, source_target_pairs={{0,4},{4,8},{8,12},{12,16},{16,20},{20,24},{24,28},{28,0},{1,5},{5... | collective-permute-start | bytes 393224 | tf_op jit(solution)/shard_map/ppermute | solution.py:326
  291.6 9.1 %collective-permute-done.24 = bf16[8,4,128,128]{3,2,1,0:T(8,128)(2,1)S(1)} collective-permute-done((bf16[8,4,128,128]{3,2,1,0:T(8,128)(2,1)S(1)}, bf16[8,4,128,128]{3,2,1,0:T(8,128)(2,1)S(1)}, u32[]{:S(2)}, u32[]{:S(2)}) %collective-permute-start.24) | collective-permute-done | bytes 1048608 | tf_op jit(solution)/shard_map/ppermute | solution.py:183
  301.4 4.6 %collective-permute-start.25 = (bf16[8,4,128,128]{3,2,1,0:T(8,128)(2,1)S(1)}, bf16[8,4,128,128]{3,2,1,0:T(8,128)(2,1)S(1)}, u32[]{:S(2)}, u32[]{:S(2)}) collective-permute-start(bf16[8,4,128,128]{3,2,1,0:T(8,128)(2,1)S(1)} %fusion.4), channel_id=1, source_target_pairs={{0,8},{4,12},{8,16},{12,20},{1,9},{5,13},{9,17},{13,21},{2,10},{6,... | collective-permute-start | bytes 3145736 | tf_op jit(solution)/shard_map/ppermute | solution.py:183
  306.0 6.9 %collective-permute-start = (bf16[128,512]{1,0:T(8,128)(2,1)S(1)}, bf16[128,512]{1,0:T(8,128)(2,1)S(1)}, u32[]{:S(2)}, u32[]{:S(2)}) collective-permute-start(bf16[128,512]{1,0:T(8,128)(2,1)S(1)} %get-tuple-element.66), channel_id=1, source_target_pairs={{0,4},{4,8},{8,12},{12,16},{16,20},{20,24},{24,28},{28,0},{1,5},{5... | collective-permute-start | bytes 393224 | tf_op jit(solution)/shard_map/ppermute | solution.py:326
  312.9 8.5 %shard_map.101 = (bf16[8,4,128,128]{3,2,1,0:T(8,128)(2,1)S(1)}, f32[8,4,128]{2,1,0:T(4,128)S(1)}) custom-call(s32[64]{0:T(128)S(1)} %get-tuple-element.104.idx_ref, s32[8]{0:T(128)S(1)} %get-tuple-element.96.cnt_ref, bf16[8,128,512]{2,1,0:T(8,128)(2,1)S(1)} %bitcast.59, bf16[16,128,1024]{2,1,0:T(8,128)(2,1)S(1)} %copy-done.3), custom_call_target="tpu_custom_call" | custom-call | flops 268435456 | bytes 16777216 | tf_op jit(solution)/shard_map/pallas_call | solution.py:110
  321.6 8.5 %shard_map.102 = (bf16[8,4,128,128]{3,2,1,0:T(8,128)(2,1)S(1)}, f32[8,4,128]{2,1,0:T(4,128)S(1)}) custom-call(s32[64]{0:T(128)S(1)} %get-tuple-element.103.idx_ref, s32[8]{0:T(128)S(1)} %get-tuple-element.95.cnt_ref, bf16[8,128,512]{2,1,0:T(8,128)(2,1)S(1)} %bitcast.62, bf16[16,128,1024]{2,1,0:T(8,128)(2,1)S(1)} %copy-done.3), custom_call_target="tpu_custom_call" | custom-call | flops 268435456 | bytes 16777216 | tf_op jit(solution)/shard_map/pallas_call | solution.py:110
  336.7 4.6 %collective-permute-start.26 = (bf16[8,4,128,128]{3,2,1,0:T(8,128)(2,1)S(1)}, bf16[8,4,128,128]{3,2,1,0:T(8,128)(2,1)S(1)}, u32[]{:S(2)}, u32[]{:S(2)}) collective-permute-start(bf16[8,4,128,128]{3,2,1,0:T(8,128)(2,1)S(1)} %add_convert_fusion.2), channel_id=1, source_target_pairs={{0,8},{4,12},{8,16},{12,20},{16,24},{20,28},{1,9},{5,13},{9,17},{1... | collective-permute-start | bytes 3145736 | tf_op jit(solution)/shard_map/ppermute | solution.py:183
  341.4 4.9 %shard_map.100 = (f32[8,4,128,128]{3,2,1,0:T(8,128)S(1)}, f32[8,4,128]{2,1,0:T(4,128)S(1)}) custom-call(bf16[1024,512]{1,0:T(8,128)(2,1)S(1)} %convolution_convert_fusion.2.q_ref, bf16[1280,512]{1,0:T(8,128)(2,1)S(1)} %pad_maximum_fusion.k0.k1.k2, bf16[1280,512]{1,0:T(8,128)(2,1)S(1)} %pad_maximum_fusion.k0.k1.k2, ...), custom_call_target="tpu_custom_call" | custom-call | flops 805306368 | bytes 10485760 | tf_op jit(solution)/shard_map/pallas_call | solution.py:50
  348.1 4.8 %collective-permute-start.27 = (f32[8,4,128]{2,1,0:T(4,128)S(1)}, f32[8,4,128]{2,1,0:T(4,128)S(1)}, u32[]{:S(2)}, u32[]{:S(2)}) collective-permute-start(f32[8,4,128]{2,1,0:T(4,128)S(1)} %get-tuple-element.68), channel_id=1, source_target_pairs={{0,8},{4,12},{8,16},{12,20},{16,24},{20,28},{1,9},{5,13},{9,17},{1... | collective-permute-start | bytes 49160 | tf_op jit(solution)/shard_map/ppermute | solution.py:183
  357.2 13.4 %collective-permute-done.35 = bf16[1024,512]{1,0:T(8,128)(2,1)S(1)} collective-permute-done((bf16[1024,512]{1,0:T(8,128)(2,1)S(1)}, bf16[1024,512]{1,0:T(8,128)(2,1)S(1)}, u32[]{:S(2)}, u32[]{:S(2)}) %collective-permute-start.35) | collective-permute-done | bytes 1048608 | tf_op jit(solution)/shard_map/ppermute | solution.py:284
  376.4 4.0 %add_convert_fusion = bf16[1024,512]{1,0:T(8,128)(2,1)} fusion(f32[1024,512]{1,0:T(8,128)S(1)} %fusion.11, f32[1024,512]{1,0:T(8,128)S(1)} %fusion.15, f32[1024,512]{1,0:T(8,128)S(1)} %fusion.13, bf16[1024,512]{1,0:T(8,128)(2,1)} %collective-permute-done.36, bf16[1024,2048]{1,0:T(8,128)(2,1)} %param.10, s32[]{:T(128)S(6)} %select_n.317, ...), kind=kOutput, calls=%fused_computation.11 | convolution fusion | flops 540016640 | bytes 9961484 | tf_op jit(solution)/shard_map/dot_general | solution.py:288
  (138 shorter events, 56.5 us)
Async XLA Ops:
  6.5 28.1 %collective-permute-start.10 = (bf16[1024,512]{1,0:T(8,128)(2,1)S(1)}, bf16[1024,512]{1,0:T(8,128)(2,1)S(1)}, u32[]{:S(2)}, u32[]{:S(2)}) collective-permute-start(bf16[1024,512]{1,0:T(8,128)(2,1)S(1)} %convolution_convert_fusion.2.q_ref), channel_id=1, source_target_pairs={{8,0},{12,4},{16,8},{20,12},{24,16},{28,20},{9,1},{13,5},{17,9},{2... | collective-permute-start | bytes 3145736 | tf_op jit(solution)/shard_map/ppermute | solution.py:214
  7.8 28.1 %collective-permute-start.7 = (bf16[1024,512]{1,0:T(8,128)(2,1)S(1)}, bf16[1024,512]{1,0:T(8,128)(2,1)S(1)}, u32[]{:S(2)}, u32[]{:S(2)}) collective-permute-start(bf16[1024,512]{1,0:T(8,128)(2,1)S(1)} %convolution_convert_fusion.2.q_ref), channel_id=1, source_target_pairs={{0,8},{4,12},{8,16},{12,20},{16,24},{20,28},{1,9},{5,13},{9,17},{1... | collective-permute-start | bytes 3145736 | tf_op jit(solution)/shard_map/ppermute | solution.py:213
  34.6 26.3 %collective-permute-start.11 = (bf16[1024,512]{1,0:T(8,128)(2,1)S(1)}, bf16[1024,512]{1,0:T(8,128)(2,1)}, u32[]{:S(2)}, u32[]{:S(2)}) collective-permute-start(bf16[1024,512]{1,0:T(8,128)(2,1)S(1)} %collective-permute-done.10), channel_id=1, source_target_pairs={{8,0},{12,4},{16,8},{20,12},{9,1},{13,5},{17,9},{21,13},{10,2},{14... | collective-permute-start | bytes 3145736 | tf_op jit(solution)/shard_map/ppermute | solution.py:214
  35.9 26.3 %collective-permute-start.8 = (bf16[1024,512]{1,0:T(8,128)(2,1)S(1)}, bf16[1024,512]{1,0:T(8,128)(2,1)}, u32[]{:S(2)}, u32[]{:S(2)}) collective-permute-start(bf16[1024,512]{1,0:T(8,128)(2,1)S(1)} %collective-permute-done.7), channel_id=1, source_target_pairs={{8,16},{12,20},{16,24},{20,28},{9,17},{13,21},{17,25},{21,29},{10,... | collective-permute-start | bytes 3145736 | tf_op jit(solution)/shard_map/ppermute | solution.py:213
  60.9 25.6 %collective-permute-start.12 = (bf16[1024,512]{1,0:T(8,128)(2,1)}, bf16[1024,512]{1,0:T(8,128)(2,1)}, u32[]{:S(2)}, u32[]{:S(2)}) collective-permute-start(bf16[1024,512]{1,0:T(8,128)(2,1)} %collective-permute-done.11), channel_id=1, source_target_pairs={{8,0},{12,4},{9,1},{13,5},{10,2},{14,6},{11,3},{15,7}} | collective-permute-start | bytes 3145736 | tf_op jit(solution)/shard_map/ppermute | solution.py:214
  62.2 24.3 %collective-permute-start.9 = (bf16[1024,512]{1,0:T(8,128)(2,1)}, bf16[1024,512]{1,0:T(8,128)(2,1)}, u32[]{:S(2)}, u32[]{:S(2)}) collective-permute-start(bf16[1024,512]{1,0:T(8,128)(2,1)} %collective-permute-done.8), channel_id=1, source_target_pairs={{16,24},{20,28},{17,25},{21,29},{18,26},{22,30},{19,27},{23,31}} | collective-permute-start | bytes 3145736 | tf_op jit(solution)/shard_map/ppermute | solution.py:213
  65.2 32.9 %collective-permute-start.19 = (bf16[1024,512]{1,0:T(8,128)(2,1)S(1)}, bf16[1024,512]{1,0:T(8,128)(2,1)}, u32[]{:S(2)}, u32[]{:S(2)}) collective-permute-start(bf16[1024,512]{1,0:T(8,128)(2,1)S(1)} %select_select_fusion.4), channel_id=1, source_target_pairs={{0,4},{4,0},{8,12},{12,8},{16,20},{20,16},{24,28},{28,24},{1,5},{5... | collective-permute-start | bytes 3145736 | tf_op jit(solution)/shard_map/ppermute | solution.py:231
  68.4 45.6 %collective-permute-start.16 = (bf16[1024,512]{1,0:T(8,128)(2,1)S(1)}, bf16[1024,512]{1,0:T(8,128)(2,1)}, u32[]{:S(2)}, u32[]{:S(2)}) collective-permute-start(bf16[1024,512]{1,0:T(8,128)(2,1)S(1)} %fusion.8), channel_id=1, source_target_pairs={{0,4},{4,0},{8,12},{12,8},{16,20},{20,16},{24,28},{28,24},{1,5},{5... | collective-permute-start | bytes 3145736 | tf_op jit(solution)/shard_map/ppermute | solution.py:231
  88.9 47.5 %collective-permute-start.13 = (bf16[1024,512]{1,0:T(8,128)(2,1)}, bf16[1024,512]{1,0:T(8,128)(2,1)}, u32[]{:S(2)}, u32[]{:S(2)}) collective-permute-start(bf16[1024,512]{1,0:T(8,128)(2,1)} %select_select_fusion.5), channel_id=1, source_target_pairs={{0,4},{4,0},{8,12},{12,8},{16,20},{20,16},{24,28},{28,24},{1,5},{5... | collective-permute-start | bytes 3145736 | tf_op jit(solution)/shard_map/ppermute | solution.py:231
  106.0 103.7 %collective-permute-start.21 = (bf16[8,4,128,128]{3,2,1,0:T(8,128)(2,1)}, bf16[8,4,128,128]{3,2,1,0:T(8,128)(2,1)}, u32[]{:S(2)}, u32[]{:S(2)}) collective-permute-start(bf16[8,4,128,128]{3,2,1,0:T(8,128)(2,1)} %get-tuple-element.52), channel_id=1, source_target_pairs={{0,4},{4,0},{8,12},{12,8},{16,20},{20,16},{24,28},{28,24},{1,5},{5... | collective-permute-start | bytes 3145736 | tf_op jit(solution)/shard_map/ppermute | solution.py:183
  119.7 90.1 %collective-permute-start.18 = (bf16[8,4,128,128]{3,2,1,0:T(8,128)(2,1)}, bf16[8,4,128,128]{3,2,1,0:T(8,128)(2,1)}, u32[]{:S(2)}, u32[]{:S(2)}) collective-permute-start(bf16[8,4,128,128]{3,2,1,0:T(8,128)(2,1)} %get-tuple-element.47), channel_id=1, source_target_pairs={{0,4},{4,0},{8,12},{12,8},{16,20},{20,16},{24,28},{28,24},{1,5},{5... | collective-permute-start | bytes 3145736 | tf_op jit(solution)/shard_map/ppermute | solution.py:183
  142.2 67.6 %collective-permute-start.15 = (bf16[8,4,128,128]{3,2,1,0:T(8,128)(2,1)}, bf16[8,4,128,128]{3,2,1,0:T(8,128)(2,1)}, u32[]{:S(2)}, u32[]{:S(2)}) collective-permute-start(bf16[8,4,128,128]{3,2,1,0:T(8,128)(2,1)} %get-tuple-element.42), channel_id=1, source_target_pairs={{0,4},{4,0},{8,12},{12,8},{16,20},{20,16},{24,28},{28,24},{1,5},{5... | collective-permute-start | bytes 3145736 | tf_op jit(solution)/shard_map/ppermute | solution.py:183
  144.4 57.2 %collective-permute-start.20 = (f32[8,4,128]{2,1,0:T(4,128)S(1)}, f32[8,4,128]{2,1,0:T(4,128)S(1)}, u32[]{:S(2)}, u32[]{:S(2)}) collective-permute-start(f32[8,4,128]{2,1,0:T(4,128)S(1)} %get-tuple-element.51), channel_id=1, source_target_pairs={{0,4},{4,0},{8,12},{12,8},{16,20},{20,16},{24,28},{28,24},{1,5},{5... | collective-permute-start | bytes 49160 | tf_op jit(solution)/shard_map/ppermute | solution.py:183
  147.0 61.2 %collective-permute-start.17 = (f32[8,4,128]{2,1,0:T(4,128)S(1)}, f32[8,4,128]{2,1,0:T(4,128)S(1)}, u32[]{:S(2)}, u32[]{:S(2)}) collective-permute-start(f32[8,4,128]{2,1,0:T(4,128)S(1)} %get-tuple-element.46), channel_id=1, source_target_pairs={{0,4},{4,0},{8,12},{12,8},{16,20},{20,16},{24,28},{28,24},{1,5},{5... | collective-permute-start | bytes 49160 | tf_op jit(solution)/shard_map/ppermute | solution.py:183
  201.6 6.6 %collective-permute-start.14 = (f32[8,4,128]{2,1,0:T(4,128)S(1)}, f32[8,4,128]{2,1,0:T(4,128)S(1)}, u32[]{:S(2)}, u32[]{:S(2)}) collective-permute-start(f32[8,4,128]{2,1,0:T(4,128)S(1)} %get-tuple-element.41), channel_id=1, source_target_pairs={{0,4},{4,0},{8,12},{12,8},{16,20},{20,16},{24,28},{28,24},{1,5},{5... | collective-permute-start | bytes 49160 | tf_op jit(solution)/shard_map/ppermute | solution.py:183
  215.1 19.1 %collective-permute-start.30 = (bf16[8,4,128,128]{3,2,1,0:T(8,128)(2,1)}, bf16[8,4,128,128]{3,2,1,0:T(8,128)(2,1)S(1)}, u32[]{:S(2)}, u32[]{:S(2)}) collective-permute-start(bf16[8,4,128,128]{3,2,1,0:T(8,128)(2,1)} %get-tuple-element.59), channel_id=1, source_target_pairs={{24,16},{28,20},{25,17},{29,21},{26,18},{30,22},{27,19},{31,23}} | collective-permute-start | bytes 3145736 | tf_op jit(solution)/shard_map/ppermute | solution.py:183
  215.8 18.4 %collective-permute-start.22 = (f32[8,4,128]{2,1,0:T(4,128)S(1)}, f32[8,4,128]{2,1,0:T(4,128)S(1)}, u32[]{:S(2)}, u32[]{:S(2)}) collective-permute-start(f32[8,4,128]{2,1,0:T(4,128)S(1)} %get-tuple-element.54), channel_id=1, source_target_pairs={{0,8},{4,12},{1,9},{5,13},{2,10},{6,14},{3,11},{7,15}} | collective-permute-start | bytes 49160 | tf_op jit(solution)/shard_map/ppermute | solution.py:183
  238.1 7.8 %collective-permute-start.31 = (bf16[8,4,128,128]{3,2,1,0:T(8,128)(2,1)S(1)}, bf16[8,4,128,128]{3,2,1,0:T(8,128)(2,1)S(1)}, u32[]{:S(2)}, u32[]{:S(2)}) collective-permute-start(bf16[8,4,128,128]{3,2,1,0:T(8,128)(2,1)S(1)} %fusion.6), channel_id=1, source_target_pairs={{16,8},{20,12},{24,16},{28,20},{17,9},{21,13},{25,17},{29,21},{18,... | collective-permute-start | bytes 3145736 | tf_op jit(solution)/shard_map/ppermute | solution.py:183
  239.0 82.7 %collective-permute-start.4 = (bf16[1024,512]{1,0:T(8,128)(2,1)S(1)}, bf16[1024,512]{1,0:T(8,128)(2,1)S(1)}, u32[]{:S(2)}, u32[]{:S(2)}) collective-permute-start(bf16[1024,512]{1,0:T(8,128)(2,1)S(1)} %convolution_convert_fusion.2.q_ref), channel_id=1, source_target_pairs={{0,4},{4,0},{8,12},{12,8},{16,20},{20,16},{24,28},{28,24},{1,5},{5... | collective-permute-start | bytes 3145736 | tf_op jit(solution)/shard_map/ppermute | solution.py:211
  248.7 52.0 %collective-permute-start.24 = (bf16[8,4,128,128]{3,2,1,0:T(8,128)(2,1)S(1)}, bf16[8,4,128,128]{3,2,1,0:T(8,128)(2,1)S(1)}, u32[]{:S(2)}, u32[]{:S(2)}) collective-permute-start(bf16[8,4,128,128]{3,2,1,0:T(8,128)(2,1)S(1)} %get-tuple-element.56), channel_id=1, source_target_pairs={{0,8},{4,12},{1,9},{5,13},{2,10},{6,14},{3,11},{7,15}} | collective-permute-start | bytes 3145736 | tf_op jit(solution)/shard_map/ppermute | solution.py:183
  282.3 39.1 %collective-permute-start.2 = (bf16[128,512]{1,0:T(8,128)(2,1)S(1)}, bf16[128,512]{1,0:T(8,128)(2,1)S(1)}, u32[]{:S(2)}, u32[]{:S(2)}) collective-permute-start(bf16[128,512]{1,0:T(8,128)(2,1)S(1)} %get-tuple-element.64), channel_id=1, source_target_pairs={{0,4},{4,8},{8,12},{12,16},{16,20},{20,24},{24,28},{28,0},{1,5},{5... | collective-permute-start | bytes 393224 | tf_op jit(solution)/shard_map/ppermute | solution.py:326
  289.2 32.3 %collective-permute-start.3 = (bf16[128,512]{1,0:T(8,128)(2,1)S(1)}, bf16[128,512]{1,0:T(8,128)(2,1)S(1)}, u32[]{:S(2)}, u32[]{:S(2)}) collective-permute-start(bf16[128,512]{1,0:T(8,128)(2,1)S(1)} %get-tuple-element.65), channel_id=1, source_target_pairs={{4,0},{8,4},{12,8},{16,12},{20,16},{24,20},{28,24},{0,28},{5,1},{9... | collective-permute-start | bytes 393224 | tf_op jit(solution)/shard_map/ppermute | solution.py:327
  301.4 33.6 %collective-permute-start.25 = (bf16[8,4,128,128]{3,2,1,0:T(8,128)(2,1)S(1)}, bf16[8,4,128,128]{3,2,1,0:T(8,128)(2,1)S(1)}, u32[]{:S(2)}, u32[]{:S(2)}) collective-permute-start(bf16[8,4,128,128]{3,2,1,0:T(8,128)(2,1)S(1)} %fusion.4), channel_id=1, source_target_pairs={{0,8},{4,12},{8,16},{12,20},{1,9},{5,13},{9,17},{13,21},{2,10},{6,... | collective-permute-start | bytes 3145736 | tf_op jit(solution)/shard_map/ppermute | solution.py:183
  306.0 25.4 %collective-permute-start = (bf16[128,512]{1,0:T(8,128)(2,1)S(1)}, bf16[128,512]{1,0:T(8,128)(2,1)S(1)}, u32[]{:S(2)}, u32[]{:S(2)}) collective-permute-start(bf16[128,512]{1,0:T(8,128)(2,1)S(1)} %get-tuple-element.66), channel_id=1, source_target_pairs={{0,4},{4,8},{8,12},{12,16},{16,20},{20,24},{24,28},{28,0},{1,5},{5... | collective-permute-start | bytes 393224 | tf_op jit(solution)/shard_map/ppermute | solution.py:326
  321.5 10.0 %collective-permute-start.1 = (bf16[128,512]{1,0:T(8,128)(2,1)S(1)}, bf16[128,512]{1,0:T(8,128)(2,1)S(1)}, u32[]{:S(2)}, u32[]{:S(2)}) collective-permute-start(bf16[128,512]{1,0:T(8,128)(2,1)S(1)} %get-tuple-element.67), channel_id=1, source_target_pairs={{4,0},{8,4},{12,8},{16,12},{20,16},{24,20},{28,24},{0,28},{5,1},{9... | collective-permute-start | bytes 393224 | tf_op jit(solution)/shard_map/ppermute | solution.py:327
  330.1 17.5 %collective-permute-start.6 = (bf16[8,4,128,128]{3,2,1,0:T(8,128)(2,1)S(1)}, bf16[8,4,128,128]{3,2,1,0:T(8,128)(2,1)S(1)}, u32[]{:S(2)}, u32[]{:S(2)}) collective-permute-start(bf16[8,4,128,128]{3,2,1,0:T(8,128)(2,1)S(1)} %get-tuple-element.34), channel_id=1, source_target_pairs={{0,4},{4,0},{8,12},{12,8},{16,20},{20,16},{24,28},{28,24},{1,5},{5... | collective-permute-start | bytes 3145736 | tf_op jit(solution)/shard_map/ppermute | solution.py:183
  331.6 14.7 %collective-permute-start.5 = (f32[8,4,128]{2,1,0:T(4,128)S(1)}, f32[8,4,128]{2,1,0:T(4,128)S(1)}, u32[]{:S(2)}, u32[]{:S(2)}) collective-permute-start(f32[8,4,128]{2,1,0:T(4,128)S(1)} %get-tuple-element.33), channel_id=1, source_target_pairs={{0,4},{4,0},{8,12},{12,8},{16,20},{20,16},{24,28},{28,24},{1,5},{5... | collective-permute-start | bytes 49160 | tf_op jit(solution)/shard_map/ppermute | solution.py:183
  333.7 20.4 %collective-permute-start.32 = (bf16[8,4,128,128]{3,2,1,0:T(8,128)(2,1)S(1)}, bf16[8,4,128,128]{3,2,1,0:T(8,128)(2,1)S(1)}, u32[]{:S(2)}, u32[]{:S(2)}) collective-permute-start(bf16[8,4,128,128]{3,2,1,0:T(8,128)(2,1)S(1)} %get-tuple-element.55), channel_id=1, source_target_pairs={{8,0},{12,4},{16,8},{20,12},{24,16},{28,20},{9,1},{13,5},{17,9},{2... | collective-permute-start | bytes 3145736 | tf_op jit(solution)/shard_map/ppermute | solution.py:183
  336.7 17.4 %collective-permute-start.26 = (bf16[8,4,128,128]{3,2,1,0:T(8,128)(2,1)S(1)}, bf16[8,4,128,128]{3,2,1,0:T(8,128)(2,1)S(1)}, u32[]{:S(2)}, u32[]{:S(2)}) collective-permute-start(bf16[8,4,128,128]{3,2,1,0:T(8,128)(2,1)S(1)} %add_convert_fusion.2), channel_id=1, source_target_pairs={{0,8},{4,12},{8,16},{12,20},{16,24},{20,28},{1,9},{5,13},{9,17},{1... | collective-permute-start | bytes 3145736 | tf_op jit(solution)/shard_map/ppermute | solution.py:183
  346.3 6.6 %collective-permute-start.33 = (f32[8,4,128]{2,1,0:T(4,128)S(1)}, f32[8,4,128]{2,1,0:T(4,128)S(1)}, u32[]{:S(2)}, u32[]{:S(2)}) collective-permute-start(f32[8,4,128]{2,1,0:T(4,128)S(1)} %get-tuple-element.53), channel_id=1, source_target_pairs={{8,0},{12,4},{16,8},{20,12},{24,16},{28,20},{9,1},{13,5},{17,9},{2... | collective-permute-start | bytes 49160 | tf_op jit(solution)/shard_map/ppermute | solution.py:183
  355.7 14.9 %collective-permute-start.35 = (bf16[1024,512]{1,0:T(8,128)(2,1)S(1)}, bf16[1024,512]{1,0:T(8,128)(2,1)S(1)}, u32[]{:S(2)}, u32[]{:S(2)}) collective-permute-start(bf16[1024,512]{1,0:T(8,128)(2,1)S(1)} %shard_map.109), channel_id=1, source_target_pairs={{0,2},{1,3},{2,0},{3,1},{4,6},{5,7},{6,4},{7,5},{8,10},{9,11},{10,... | collective-permute-start | bytes 3145736 | tf_op jit(solution)/shard_map/ppermute | solution.py:284
  357.2 17.3 %collective-permute-start.34 = (bf16[1024,512]{1,0:T(8,128)(2,1)S(1)}, bf16[1024,512]{1,0:T(8,128)(2,1)S(1)}, u32[]{:S(2)}, u32[]{:S(2)}) collective-permute-start(bf16[1024,512]{1,0:T(8,128)(2,1)S(1)} %shard_map.109), channel_id=1, source_target_pairs={{0,1},{1,0},{2,3},{3,2},{4,5},{5,4},{6,7},{7,6},{8,9},{9,8},{10,11... | collective-permute-start | bytes 3145736 | tf_op jit(solution)/shard_map/ppermute | solution.py:284
  (27 other events, 320.8 us)
